TPU v7x, 32 devices: a whole 2x2x4 slice. The times are simulated.
32 devices in a mesh: ctx: 16 (over z, y, core), head: 2 (over x).
Axes of the slice: x: 2, y: 2, z: 4, core: 2. Of those that a mesh axis runs over, the one named last changes fastest.
Arguments:
- query1: bfloat16 [8192, 6144], P('ctx', 'head'), may hold values from -6 to 6
- key1: bfloat16 [8192, 6144], P('ctx', 'head'), may hold values from -6 to 6
- value1: bfloat16 [8192, 6144], P('ctx', 'head'), may hold values from -50 to 50
- log_decay: float32 [8192, 64], P('ctx', 'head'), may hold values from -1 to 0
- out_weight: bfloat16 [6144, 3072], P('head'), may hold values from -0.078125 to 0.078125
- query2: bfloat16 [8192, 6144], P('ctx', 'head'), may hold values from -12 to 12
- key2: bfloat16 [8192, 6144], P('ctx', 'head'), may hold values from -6 to 6
- value2: bfloat16 [8192, 6144], P('ctx', 'head'), may hold values from -6 to 6
Outputs:
- linear_mixed: bfloat16 [8192, 3072], P(('ctx', 'head'))
- attended: bfloat16 [8192, 6144], P('ctx', 'head')
All inputs are finite; a program needn't handle non-finite values.
Results may differ from a plain program's by a relative error of at most 0.017.
Values may be sent and summed in bfloat16 or wider, within the bound.
No kernel may reach another device: no remote copies, remote signals or barrier semaphores. Data moves between devices by JAX's collectives and lax.ppermute only.
A program may use at most 320 MiB of HBM per device.

v0:
```python
import functools
import math

import jax
import jax.numpy as jnp
from jax import lax
from jax.experimental import pallas as pl
from jax.experimental.pallas import tpu as pltpu
from jax.sharding import PartitionSpec as P

DH = 96
SUB = 256
BUNDLE = 4
WIDE = BUNDLE * DH
LANES = 128
EPS_NORM = 1e-06
VMEM_BYTES = 60 * 1024 * 1024
WINDOWS = ((0, 128, 0), (0, 256, 96), (128, 256, 64), (256, 128, 32))


def cheap():
    return pl.CostEstimate(flops=1000, bytes_accessed=1000, transcendentals=0)


def params():
    return pltpu.CompilerParams(vmem_limit_bytes=VMEM_BYTES)


def untouched(deps):
    return [pl.BlockSpec(memory_space=pltpu.HBM)] * len(deps)


def gate_kernel(*refs):
    del refs


def gate(value, deps):
    return pl.pallas_call(
        gate_kernel,
        in_specs=untouched([value, *deps]),
        out_specs=pl.BlockSpec(memory_space=pltpu.HBM),
        out_shape=jax.ShapeDtypeStruct(value.shape, value.dtype),
        input_output_aliases={0: 0},
        compiler_params=params(),
        cost_estimate=cheap(),
        name="gate",
    )(value, *deps)


def head_lanes(shape, start):
    lane = lax.broadcasted_iota(jnp.int32, shape, len(shape) - 1)
    return (lane >= start) & (lane < start + DH)


def pack_kernel(key_ref, value_ref, *rest):
    out_ref = rest[-1]
    out_ref[0] = key_ref[...]
    out_ref[1] = value_ref[...]


def pack(key, value, base, bundles, deps):
    rows = key.shape[0]
    block = pl.BlockSpec((rows, WIDE), lambda b: (0, base + b))
    return pl.pallas_call(
        pack_kernel,
        grid=(bundles,),
        in_specs=[block, block] + untouched(deps),
        out_specs=pl.BlockSpec((2, rows, WIDE), lambda b: (0, 0, b)),
        out_shape=jax.ShapeDtypeStruct((2, rows, bundles * WIDE), key.dtype),
        compiler_params=params(),
        cost_estimate=cheap(),
        name="pack",
    )(key, value, *deps)


def pick_kernel(info, chip_ref, back_ref, *rest):
    out_ref = rest[-1]
    from_back = lax.rem(info[0], 4) == 1

    @pl.when(from_back)
    def _():
        out_ref[...] = back_ref[...]

    @pl.when(jnp.logical_not(from_back))
    def _():
        out_ref[...] = chip_ref[...]


def pick(info, chip, back, deps):
    _, rows, width = chip.shape
    shape = (2, rows, WIDE)

    def from_chip(b, info):
        return (0, 0, jnp.where(lax.rem(info[0], 4) == 1, 0, b))

    def from_back(b, info):
        return (0, 0, jnp.where(lax.rem(info[0], 4) == 1, b, 0))

    return pl.pallas_call(
        pick_kernel,
        grid_spec=pltpu.PrefetchScalarGridSpec(
            num_scalar_prefetch=1,
            grid=(width // WIDE,),
            in_specs=[pl.BlockSpec(shape, from_chip), pl.BlockSpec(shape, from_back)]
            + untouched(deps),
            out_specs=pl.BlockSpec(shape, lambda b, _: (0, 0, b)),
        ),
        out_shape=jax.ShapeDtypeStruct(chip.shape, chip.dtype),
        compiler_params=params(),
        cost_estimate=cheap(),
        name="pick",
    )(info, chip, back, *deps)


def attend_body(exists, query_ref, slots, out_ref):
    rows = query_ref.shape[0]
    scale = math.log2(math.e) / math.sqrt(DH)
    row = lax.broadcasted_iota(jnp.int32, (SUB, SUB), 0)
    col = lax.broadcasted_iota(jnp.int32, (SUB, SUB), 1)
    newer, older = col > row, col <= row
    low = jnp.float32(-1e30)
    units = [(part, window) for part in range(rows // SUB) for window in WINDOWS]

    def spans(part):
        first = part * SUB
        return [(first, rows), (0, rows), (0, rows), (0, first + SUB)]

    def score_unit(part, window):
        start, width, place = window
        lanes = slice(start, start + width)
        query = query_ref[part * SUB : (part + 1) * SUB, lanes]
        query = jnp.where(head_lanes(query.shape, place), query, jnp.zeros_like(query))
        tiles, peak = [], None
        for slot in range(4):
            begin, end = spans(part)[slot]
            tiles.append([])
            top = None
            for at in range(begin, end, SUB):
                score = lax.dot_general(
                    query,
                    slots[slot][0][at : at + SUB, lanes],
                    (((1,), (1,)), ((), ())),
                    preferred_element_type=jnp.float32,
                )
                if slot == 0 and at == begin:
                    score = jnp.where(newer, score, low)
                if slot == 3 and at == end - SUB:
                    score = jnp.where(older, score, low)
                tiles[slot].append(score)
                for lane in range(0, SUB, LANES):
                    piece = score[:, lane : lane + LANES]
                    top = piece if top is None else jnp.maximum(top, piece)
            if slot < 3:
                top = jnp.where(exists[slot], top, low)
            peak = top if peak is None else jnp.maximum(peak, top)
        return tiles, jnp.max(peak, axis=1, keepdims=True) * scale

    def value_unit(part, window, tiles, peak):
        start, width, place = window
        lanes = slice(start, start + width)
        result = None
        for slot in range(4):
            begin, end = spans(part)[slot]
            shift = peak
            if slot < 3:
                shift = jnp.where(exists[slot], peak, jnp.float32(1e30))
            for index, at in enumerate(range(begin, end, SUB)):
                weight = jnp.exp2(tiles[slot][index] * scale - shift).astype(jnp.bfloat16)
                value = slots[slot][1][at : at + SUB, lanes]
                value = jnp.where(head_lanes(value.shape, place), value, jnp.ones_like(value))
                term = jnp.dot(weight, value, preferred_element_type=jnp.float32)
                result = term if result is None else result + term
        spare = 96 if place == 0 else 0
        result = result * (1.0 / result[:, spare : spare + 1])
        return jnp.where(head_lanes(result.shape, place), result, 0.0)

    ready = score_unit(*units[0])
    tiles_out = [None] * (WIDE // LANES)
    for index, (part, window) in enumerate(units):
        following = score_unit(*units[index + 1]) if index + 1 < len(units) else None
        result = value_unit(part, window, *ready)
        for lane in range(0, window[1], LANES):
            place = (window[0] + lane) // LANES
            piece = result[:, lane : lane + LANES]
            tiles_out[place] = piece if tiles_out[place] is None else tiles_out[place] + piece
        if window is WINDOWS[-1]:
            for place, piece in enumerate(tiles_out):
                out_ref[
                    part * SUB : (part + 1) * SUB, place * LANES : (place + 1) * LANES
                ] = piece.astype(out_ref.dtype)
            tiles_out = [None] * (WIDE // LANES)
        ready = following


def attend_kernel(info, query_ref, key_ref, value_ref, near_ref, mid_ref, swap_ref, *rest):
    out_ref = rest[-1]
    position = info[0]
    exists = [position >= 3, position >= 2, position >= 1]
    own = (key_ref, value_ref)
    near, mid, swap = [(r.at[0], r.at[1]) for r in (near_ref, mid_ref, swap_ref)]
    core = lax.rem(position, 2)

    @pl.when(core == 0)
    def _():
        attend_body(exists, query_ref, [near, mid, swap, own], out_ref)

    @pl.when(core == 1)
    def _():
        attend_body(exists, query_ref, [swap, mid, near, own], out_ref)


def attend(info, query, key, value, near, mid, swap, out, base, deps):
    rows = query.shape[0]
    block = pl.BlockSpec((rows, WIDE), lambda b, _: (0, base + b))
    pair = pl.BlockSpec((2, rows, WIDE), lambda b, _: (0, 0, b))
    filled = [] if out is None else [out]
    return pl.pallas_call(
        attend_kernel,
        grid_spec=pltpu.PrefetchScalarGridSpec(
            num_scalar_prefetch=1,
            grid=(near.shape[2] // WIDE,),
            in_specs=[block, block, block, pair, pair, pair] + untouched([*filled, *deps]),
            out_specs=block,
        ),
        out_shape=jax.ShapeDtypeStruct(query.shape, query.dtype),
        input_output_aliases={7: 0} if filled else {},
        compiler_params=params(),
        cost_estimate=cheap(),
        name="attend",
    )(info, query, key, value, near, mid, swap, *filled, *deps)


def opened(message):
    wide = message.astype(jnp.float32)
    lane = lax.broadcasted_iota(jnp.int32, wide.shape, wide.ndim - 1)
    return jnp.where(lane == DH, wide + wide[..., DH + 1 : DH + 2], wide)


def closed(exact):
    lane = lax.broadcasted_iota(jnp.int32, exact.shape, exact.ndim - 1)
    decay = exact[..., DH : DH + 1]
    rest = decay - decay.astype(jnp.bfloat16).astype(jnp.float32)
    return jnp.where(lane == DH + 1, rest, exact).astype(jnp.bfloat16)


def joined(earlier, later):
    lane = lax.broadcasted_iota(jnp.int32, earlier.shape, earlier.ndim - 1)
    kept = jnp.exp(later[..., DH : DH + 1])
    return jnp.where(lane == DH, earlier + later, earlier * kept + later)


def state_kernel(key_ref, value_ref, decay_ref, *rest):
    exact_ref, first_ref, sent_ref = rest[-3:]
    rows = key_ref.shape[0]
    lane = lax.broadcasted_iota(jnp.int32, (DH, LANES), 1)
    key_t = key_ref[...].T
    for head, (start, width, place) in enumerate(WINDOWS):
        lanes = slice(start, start + width)
        state, before = None, None
        for at in range(0, rows, SUB):
            running = decay_ref[0, at : at + SUB, head : head + 1]
            anchor = running[SUB - 1 :, :]
            value = value_ref[at : at + SUB, lanes].astype(jnp.float32) * jnp.exp(anchor - running)
            update = jnp.dot(
                key_t[head * DH : (head + 1) * DH, at : at + SUB],
                value.astype(jnp.bfloat16),
                preferred_element_type=jnp.float32,
            )
            if at + SUB == rows:
                first_ref[head] = narrow(state, place)
            state = update if state is None else state * jnp.exp(anchor - before) + update
            before = anchor
        exact = jnp.where(lane == DH, before, narrow(state, place))
        exact_ref[head] = exact
        sent_ref[head] = closed(exact)


def narrow(state, place):
    width = state.shape[1]
    if place:
        state = pltpu.roll(state, width - place, axis=1)
    state = state[:, :LANES]
    lane = lax.broadcasted_iota(jnp.int32, state.shape, 1)
    return jnp.where(lane < DH, state, 0.0)


def widen(state, width, place):
    lane = lax.broadcasted_iota(jnp.int32, state.shape, 1)
    state = jnp.where(lane < DH, state, 0.0)
    if width > LANES:
        state = jnp.concatenate([state, jnp.zeros((DH, width - LANES), jnp.float32)], axis=1)
    if place:
        state = pltpu.roll(state, place, axis=1)
    pads = []
    if place:
        pads.append(jnp.zeros((place, width), jnp.float32))
    pads.append(state)
    if place + DH < width:
        pads.append(jnp.zeros((width - place - DH, width), jnp.float32))
    return jnp.concatenate(pads, axis=0).astype(jnp.bfloat16)


def local_state(key, value, decay_cols, deps):
    rows, width = key.shape
    bundles = width // WIDE
    block = pl.BlockSpec((rows, WIDE), lambda b: (0, b))
    out = pl.BlockSpec((BUNDLE, DH, LANES), lambda b: (b, 0, 0))
    shape = (bundles * BUNDLE, DH, LANES)
    return pl.pallas_call(
        state_kernel,
        grid=(bundles,),
        in_specs=[block, block, pl.BlockSpec((1, rows, BUNDLE), lambda b: (b, 0, 0))]
        + untouched(deps),
        out_specs=[out, out, out],
        out_shape=[
            jax.ShapeDtypeStruct(shape, jnp.float32),
            jax.ShapeDtypeStruct(shape, jnp.float32),
            jax.ShapeDtypeStruct(shape, jnp.bfloat16),
        ],
        compiler_params=params(),
        cost_estimate=cheap(),
        name="local_state",
    )(key, value, decay_cols, *deps)


def chip_state_kernel(info, exact_ref, other_ref, *rest):
    chip_ref, sent_ref = rest[-2:]
    even = lax.rem(info[0], 2) == 0
    mine, other = exact_ref[...], opened(other_ref[...])
    chip = joined(jnp.where(even, mine, other), jnp.where(even, other, mine))
    chip_ref[...] = chip
    sent_ref[...] = closed(chip)


def chip_state(info, exact, other, deps):
    half = exact.shape[0] // 2
    shape = (half, DH, LANES)
    block = pl.BlockSpec((BUNDLE, DH, LANES), lambda b, _: (b, 0, 0))
    steps = half // BUNDLE

    def mine(b, info):
        return (lax.rem(info[0], 2) * steps + b, 0, 0)

    return pl.pallas_call(
        chip_state_kernel,
        grid_spec=pltpu.PrefetchScalarGridSpec(
            num_scalar_prefetch=1,
            grid=(steps,),
            in_specs=[pl.BlockSpec((BUNDLE, DH, LANES), mine)] * 2 + untouched(deps),
            out_specs=[block, block],
        ),
        out_shape=[
            jax.ShapeDtypeStruct(shape, jnp.float32),
            jax.ShapeDtypeStruct(shape, jnp.bfloat16),
        ],
        compiler_params=params(),
        cost_estimate=cheap(),
        name="chip_state",
    )(info, exact, other, *deps)


def join_kernel(start, last, chip_ref, before_ref, arrived_ref, *rest):
    chip_out, before_out, sent_ref = rest[-3:]
    arrived = opened(arrived_ref[...])
    before = arrived if start else joined(arrived, before_ref[...])
    before_out[...] = before
    if last:
        sent_ref[...] = closed(before)
    else:
        chip = joined(arrived, chip_ref[...])
        chip_out[...] = chip
        sent_ref[...] = closed(chip)


def join(chip, before, arrived, start, last, deps):
    block = pl.BlockSpec((BUNDLE, DH, LANES), lambda b: (b, 0, 0))
    return pl.pallas_call(
        functools.partial(join_kernel, start, last),
        grid=(chip.shape[0] // BUNDLE,),
        in_specs=[block] * 3 + untouched(deps),
        out_specs=[block] * 3,
        out_shape=[
            jax.ShapeDtypeStruct(chip.shape, jnp.float32),
            jax.ShapeDtypeStruct(chip.shape, jnp.float32),
            jax.ShapeDtypeStruct(chip.shape, jnp.bfloat16),
        ],
        compiler_params=params(),
        cost_estimate=cheap(),
        name="join",
    )(chip, before, arrived, *deps)


def spread(result, start, tiles_out):
    for lane in range(0, result.shape[1], LANES):
        tile = (start + lane) // LANES
        piece = result[:, lane : lane + LANES]
        tiles_out[tile] = piece if tiles_out[tile] is None else tiles_out[tile] + piece


def mix_local_kernel(query_ref, key_ref, value_ref, col_ref, row_ref, first_ref, *rest):
    out_ref = rest[-1]
    rows = query_ref.shape[0]
    row = lax.broadcasted_iota(jnp.int32, (SUB, SUB), 0)
    col = lax.broadcasted_iota(jnp.int32, (SUB, SUB), 1)
    causal = col <= row
    for at in range(0, rows, SUB):
        here = slice(at, at + SUB)
        tiles_out = [None] * (WIDE // LANES)
        for head, (start, width, place) in enumerate(WINDOWS):
            lanes = slice(start, start + width)
            query = query_ref[here, lanes]
            query = jnp.where(head_lanes(query.shape, place), query, jnp.zeros_like(query))
            down = col_ref[0, here, head : head + 1]
            score = lax.dot_general(
                query,
                key_ref[here, lanes],
                (((1,), (1,)), ((), ())),
                preferred_element_type=jnp.float32,
            )
            gap = jnp.where(causal, down - row_ref[0, head : head + 1, here], -jnp.inf)
            mixing = (score * jnp.exp(gap)).astype(jnp.bfloat16)
            result = jnp.dot(mixing, value_ref[here, lanes], preferred_element_type=jnp.float32)
            if at:
                since = down - col_ref[0, at - 1 : at, head : head + 1]
                scaled = (query.astype(jnp.float32) * jnp.exp(since)).astype(jnp.bfloat16)
                result = result + jnp.dot(
                    scaled, widen(first_ref[head], width, place), preferred_element_type=jnp.float32
                )
            spread(jnp.where(head_lanes(result.shape, place), result, 0.0), start, tiles_out)
        for tile, piece in enumerate(tiles_out):
            out_ref[here, tile * LANES : (tile + 1) * LANES] = piece


def mix_local(query, key, value, decay_cols, decay_rows, first, deps):
    rows, width = query.shape
    block = pl.BlockSpec((rows, WIDE), lambda b: (0, b))
    return pl.pallas_call(
        mix_local_kernel,
        grid=(width // WIDE,),
        in_specs=[
            block,
            block,
            block,
            pl.BlockSpec((1, rows, BUNDLE), lambda b: (b, 0, 0)),
            pl.BlockSpec((1, BUNDLE, rows), lambda b: (b, 0, 0)),
            pl.BlockSpec((BUNDLE, DH, LANES), lambda b: (b, 0, 0)),
        ]
        + untouched(deps),
        out_specs=block,
        out_shape=jax.ShapeDtypeStruct((rows, width), jnp.float32),
        compiler_params=params(),
        cost_estimate=cheap(),
        name="mix_local",
    )(query, key, value, decay_cols, decay_rows, first, *deps)


def mix_final_kernel(half, info, query_ref, local_ref, col_ref, own_ref, sent_ref, other_ref, *rest):
    out_ref = rest[-1]
    rows = query_ref.shape[0]
    core = lax.rem(info[0], 2)
    mine = (pl.program_id(0) >= half).astype(jnp.int32) == core
    states = []
    for head, (_, width, place) in enumerate(WINDOWS):
        state = jnp.where(mine, own_ref[head], opened(sent_ref[head]))
        state = jnp.where(core == 0, state, joined(state, opened(other_ref[head])))
        states.append(widen(state, width, place))
    for at in range(0, rows, SUB):
        here = slice(at, at + SUB)
        tiles_out = [None] * (WIDE // LANES)
        for head, (start, width, place) in enumerate(WINDOWS):
            lanes = slice(start, start + width)
            inside = head_lanes((SUB, width), place)
            query = jnp.where(inside, query_ref[here, lanes].astype(jnp.float32), 0.0)
            scaled = (query * jnp.exp(col_ref[0, here, head : head + 1])).astype(jnp.bfloat16)
            result = jnp.dot(scaled, states[head], preferred_element_type=jnp.float32)
            result = jnp.where(inside, result + local_ref[here, lanes], 0.0)
            square = jnp.sum(result * result, axis=1, keepdims=True) * (1.0 / DH)
            spread(result * lax.rsqrt(square + EPS_NORM), start, tiles_out)
        for tile, piece in enumerate(tiles_out):
            out_ref[here, tile * LANES : (tile + 1) * LANES] = piece.astype(out_ref.dtype)


def mix_final(info, query, local, decay_cols, own, sent, other, deps):
    rows, width = query.shape
    bundles = width // WIDE
    half = bundles // 2
    block = pl.BlockSpec((rows, WIDE), lambda b, _: (0, b))
    states = pl.BlockSpec((BUNDLE, DH, LANES), lambda b, _: (b, 0, 0))
    halves = pl.BlockSpec((BUNDLE, DH, LANES), lambda b, _: (lax.rem(b, half), 0, 0))
    return pl.pallas_call(
        functools.partial(mix_final_kernel, half),
        grid_spec=pltpu.PrefetchScalarGridSpec(
            num_scalar_prefetch=1,
            grid=(bundles,),
            in_specs=[
                block,
                block,
                pl.BlockSpec((1, rows, BUNDLE), lambda b, _: (b, 0, 0)),
                halves,
                halves,
                states,
            ]
            + untouched(deps),
            out_specs=block,
        ),
        out_shape=jax.ShapeDtypeStruct((rows, width), jnp.bfloat16),
        compiler_params=params(),
        cost_estimate=cheap(),
        name="mix_final",
    )(info, query, local, decay_cols, own, sent, other, *deps)


def group_sizes(bundles):
    if bundles == 8:
        return [2, 3, 2, 1]
    return [1] * bundles


def per_device(query1, key1, value1, log_decay, out_weight, query2, key2, value2):
    rows, width = query1.shape
    bundles = width // WIDE
    count = lax.axis_size("ctx")
    position = lax.axis_index("ctx")
    info = jnp.full((1,), position, jnp.int32)

    def moved(value, pairs):
        return lax.ppermute(value, "ctx", [(s, t) for s, t in pairs if 0 <= t < count])

    everyone = range(count)
    step_pairs = [(s, s + 3 if s % 2 else s + 1) for s in everyone]
    chip_pairs = [(s, s + 2) for s in everyone if s % 4 != 3]
    back_pairs = [(s, s - 1) for s in everyone if s % 4 == 2 and s > 2]
    swap_pairs = [(s, s ^ 1) for s in everyone]

    sizes = group_sizes(bundles)
    groups = len(sizes)
    bases = [sum(sizes[:g]) for g in range(groups)]
    near, chip, back, mid, swap = {}, {}, {}, {}, {}
    done = {"last": [], "attended": None}

    def do_pack(group):
        if group < groups:
            sent = pack(key2, value2, bases[group], sizes[group], done["last"])
            near[group] = moved(sent, step_pairs)
            chip[group] = moved(sent, chip_pairs)
            done["last"] = [sent]

    def do_back(group):
        if group < groups:
            near[group] = gate(near[group], done["last"])
            back[group] = moved(near[group], back_pairs)

    def do_pick(group):
        if group < groups:
            mid[group] = pick(info, chip[group], back[group], done["last"])
            swap[group] = moved(mid[group], swap_pairs)
            done["last"] = [mid[group]]

    def do_attend(group):
        if group < groups:
            done["attended"] = attend(
                info, query2, key2, value2, near[group], mid[group], swap[group],
                done["attended"], bases[group], done["last"],
            )
            done["last"] = [done["attended"]]

    light = {"distance": 1, "before": None}

    def do_state():
        running = jnp.cumsum(log_decay, axis=0)
        light["cols"] = running.reshape(rows, bundles, BUNDLE).transpose(1, 0, 2)
        light["rows"] = running.T.reshape(bundles, BUNDLE, rows)
        exact, first, sent = local_state(key1, value1, light["cols"], done["last"])
        light["first"] = first
        light["other"] = moved(sent, swap_pairs)
        light["exact"] = exact
        done["last"] = [sent]

    def do_chip():
        light["chip"], sent = chip_state(info, light["exact"], light["other"], done["last"])
        light["arrived"] = moved(sent, [(s, s + 2) for s in everyone])
        light["distance"] = 1
        done["last"] = [sent]

    def do_join():
        if light["distance"] < count // 2:
            start = light["distance"] == 1
            light["distance"] *= 2
            last = light["distance"] >= count // 2
            before = light["chip"] if start else light["before"]
            light["chip"], light["before"], sent = join(
                light["chip"], before, light["arrived"], start, last, done["last"]
            )
            pairs = swap_pairs if last else [(s, s + 2 * light["distance"]) for s in everyone]
            light["arrived"] = moved(sent, pairs)
            done["last"] = [sent]

    def do_mix_local():
        light["local"] = mix_local(
            query1, key1, value1, light["cols"], light["rows"], light["first"], done["last"]
        )
        done["last"] = [light["local"]]

    def do_mix_final():
        while light["distance"] < count // 2:
            do_join()
        light["normed"] = mix_final(
            info, query1, light["local"], light["cols"], light["before"], light["arrived"],
            light["other"], done["last"],
        )
        done["last"] = [light["normed"]]

    def do_project():
        product = jnp.dot(light["normed"], out_weight, preferred_element_type=jnp.float32)
        product = product.astype(jnp.bfloat16)
        done["linear"] = lax.psum_scatter(product, "head", scatter_dimension=0, tiled=True)
        done["last"] = [product]

    def wait_chip(group):
        done["last"] = done["last"] + [chip[group]]

    do_pack(0)
    do_state()
    do_pack(1)
    do_back(0)
    do_mix_local()
    wait_chip(0)
    do_chip()
    do_pick(0)
    do_join()
    do_attend(0)
    do_join()
    do_back(1)
    wait_chip(1)
    do_join()
    do_pack(2)
    do_mix_final()
    do_pick(1)
    do_project()
    do_back(2)
    do_pack(3)
    do_attend(1)
    do_back(3)
    do_pick(2)
    do_pick(3)
    do_attend(2)
    do_attend(3)
    return (done["linear"], done["attended"])


def solution(mesh):
    in_specs = (
        P("ctx", "head"),
        P("ctx", "head"),
        P("ctx", "head"),
        P("ctx", "head"),
        P("head", None),
        P("ctx", "head"),
        P("ctx", "head"),
        P("ctx", "head"),
    )
    out_specs = (P(("ctx", "head"), None), P("ctx", "head"))
    return jax.shard_map(
        per_device, mesh=mesh, in_specs=in_specs, out_specs=out_specs, check_vma=False
    )
```

profile of v0, /device:TPU:25, one launch (start us, length us, event | category | flops | bytes accessed | tf_op | source)
XLA Modules:
  0.0 346.5 jit_solution(14562903511100333811)
XLA Ops:
  7.2 2.3 pack.4.rest_0_
  9.6 1.3 collective-permute-start.3
  10.9 3.2 collective-permute-start.1
  14.1 1.2 reduce-window.6
  15.3 0.2 slice_reduce_fusion
  15.5 0.1 bitcast_bitcast_fusion
  15.6 2.0 copy.21
  17.6 12.2 %local_state.1 = (f32[32,96,128]{2,1,0:T(8,128)}, f32[32,96,128]{2,1,0:T(8,128)}, bf16[32,96,128]{2,1,0:T(8,128)(2,1)}) custom-call(bf16[512,3072]{1,0:T(8,128)(2,1)} %key_ref.13, bf16[512,3072]{1,0:T(8,128)(2,1)} %value_ref.13, f32[8,512,4]{2,1,0:T(8,128)} %bitcast.19, bf16[2,512,768]{2,1,0:T(8,128)(2,1)} %pack.4.rest_0_), custom_call_target="tpu_custom_call" | custom-call | flops 1000 | bytes 1000 | tf_op jit(solution)/shard_map/local_state/pallas_call | solution.py:309
  29.8 3.9 %pack.5.rest_0_.refs_1_ = bf16[2,512,1152]{2,1,0:T(8,128)(2,1)} custom-call(bf16[512,3072]{1,0:T(8,128)(2,1)} %key_ref.19, bf16[512,3072]{1,0:T(8,128)(2,1)} %value_ref.19, bf16[32,96,128]{2,1,0:T(8,128)(2,1)} %get-tuple-element.16.rest_0_), custom_call_target="tpu_custom_call" | custom-call | flops 1000 | bytes 1000 | tf_op jit(solution)/shard_map/pack/pallas_call | solution.py:64
  33.7 1.1 copy-done.4
  34.9 1.3 collective-permute-start.4
  36.1 2.1 collective-permute-start
  38.2 16.5 %collective-permute-start.8 = (bf16[2,512,1152]{2,1,0:T(8,128)(2,1)}, bf16[2,512,1152]{2,1,0:T(8,128)(2,1)}, u32[]{:S(2)}, u32[]{:S(2)}) collective-permute-start(bf16[2,512,1152]{2,1,0:T(8,128)(2,1)} %pack.5.rest_0_.refs_1_), channel_id=1, source_target_pairs={{0,4},{2,6},{4,8},{8,12},{10,14},{12,16},{16,20},{18,22},{20,24},{... | collective-permute-start | bytes 7077896 | tf_op jit(solution)/shard_map/ppermute | solution.py:527
  54.7 0.1 broadcast_add_fusion
  54.8 0.7 reduce_window_sum.21.row_ref
  55.5 13.9 %mix_local.1.rest_0_.local_ref = f32[512,3072]{1,0:T(8,128)} custom-call(bf16[512,3072]{1,0:T(8,128)(2,1)} %query_ref.8, bf16[512,3072]{1,0:T(8,128)(2,1)} %key_ref.13, bf16[512,3072]{1,0:T(8,128)(2,1)} %value_ref.13, f32[8,512,4]{2,1,0:T(8,128)} %bitcast.20, f32[8,4,512]{2,1,0:T(4,128)} %reduce_window_sum.21.row_ref, ...), custom_call_target="tpu_custom_call" | custom-call | flops 1000 | bytes 1000 | tf_op jit(solution)/shard_map/mix_local/pallas_call | solution.py:437
  69.4 0.9 copy-done.8
  70.3 0.5 copy-done.3
  70.8 3.9 %chip_state.1 = (f32[16,96,128]{2,1,0:T(8,128)}, bf16[16,96,128]{2,1,0:T(8,128)(2,1)}) custom-call(s32[1]{0:T(128)} %bitcast.info, f32[32,96,128]{2,1,0:T(8,128)} %get-tuple-element.17.exact_ref, bf16[32,96,128]{2,1,0:T(8,128)(2,1)} %copy-done.8, f32[512,3072]{1,0:T(8,128)} %mix_local.1.rest_0_.local_ref, bf16[2,512,768]{2,1,0:T(8,128)(2,1)} %copy-done.3), custom_call_target="tpu_custom_call" | custom-call | flops 1000 | bytes 1000 | tf_op jit(solution)/shard_map/chip_state/pallas_call | solution.py:344
  74.7 19.1 %collective-permute-done.4.back_ref = bf16[2,512,768]{2,1,0:T(8,128)(2,1)} collective-permute-done((bf16[2,512,768]{2,1,0:T(8,128)(2,1)}, bf16[2,512,768]{2,1,0:T(8,128)(2,1)}, u32[]{:S(2)}, u32[]{:S(2)}) %collective-permute-start.4) | collective-permute-done | bytes 1572896 | tf_op jit(solution)/shard_map/ppermute | solution.py:527
  93.7 2.7 pick.4.rest_0_.mid_ref
  96.5 1.3 collective-permute-start.11
  97.8 1.9 collective-permute-start.2
  99.7 38.8 %collective-permute-done.2.arrived_ref = bf16[16,96,128]{2,1,0:T(8,128)(2,1)S(1)} collective-permute-done((bf16[16,96,128]{2,1,0:T(8,128)(2,1)S(1)}, bf16[16,96,128]{2,1,0:T(8,128)(2,1)S(1)}, u32[]{:S(2)}, u32[]{:S(2)}) %collective-permute-start.2) | collective-permute-done | bytes 393248 | tf_op jit(solution)/shard_map/ppermute | solution.py:527
  138.5 0.8 copy-done.15
  139.2 3.9 %join.3 = (f32[16,96,128]{2,1,0:T(8,128)}, f32[16,96,128]{2,1,0:T(8,128)}, bf16[16,96,128]{2,1,0:T(8,128)(2,1)}) custom-call(f32[16,96,128]{2,1,0:T(8,128)} %get-tuple-element.18.chip_ref.before_ref, f32[16,96,128]{2,1,0:T(8,128)} %get-tuple-element.18.chip_ref.before_ref, bf16[16,96,128]{2,1,0:T(8,128)(2,1)} %copy-done.15, ...), custom_call_target="tpu_custom_call" | custom-call | flops 1000 | bytes 1000 | tf_op jit(solution)/shard_map/join/pallas_call | solution.py:377
  143.1 1.5 collective-permute-start.5
  144.6 14.5 %attend.4.rest_0_ = bf16[512,3072]{1,0:T(8,128)(2,1)} custom-call(s32[1]{0:T(128)} %bitcast.info, bf16[512,3072]{1,0:T(8,128)(2,1)} %query_ref.11, bf16[512,3072]{1,0:T(8,128)(2,1)} %key_ref.19, bf16[512,3072]{1,0:T(8,128)(2,1)} %value_ref.19, bf16[2,512,768]{2,1,0:T(8,128)(2,1)} %gate.4.near_ref, bf16[2,512,768]{2,1,0:T(8,128)(2,1)} %pick.4.rest_0_.mid_ref, ...), custom_call_target="tpu_custom_call" | custom-call | flops 1000 | bytes 1000 | tf_op jit(solution)/shard_map/attend/pallas_call | solution.py:217
  159.1 0.7 copy-done.13
  159.9 4.5 %join.4 = (f32[16,96,128]{2,1,0:T(8,128)}, f32[16,96,128]{2,1,0:T(8,128)}, bf16[16,96,128]{2,1,0:T(8,128)(2,1)}) custom-call(f32[16,96,128]{2,1,0:T(8,128)} %get-tuple-element.20.chip_ref, f32[16,96,128]{2,1,0:T(8,128)} %get-tuple-element.21.before_ref, bf16[16,96,128]{2,1,0:T(8,128)(2,1)} %copy-done.13, bf16[512,3072]{1,0:T(8,128)(2,1)} %attend.4.rest_0_), custom_call_target="tpu_custom_call" | custom-call | flops 1000 | bytes 1000 | tf_op jit(solution)/shard_map/join/pallas_call | solution.py:377
  164.3 1.3 collective-permute-start.7
  165.6 12.5 %collective-permute-done.7.arrived_ref = bf16[16,96,128]{2,1,0:T(8,128)(2,1)S(1)} collective-permute-done((bf16[16,96,128]{2,1,0:T(8,128)(2,1)}, bf16[16,96,128]{2,1,0:T(8,128)(2,1)S(1)}, u32[]{:S(2)}, u32[]{:S(2)}) %collective-permute-start.7) | collective-permute-done | bytes 393248 | tf_op jit(solution)/shard_map/ppermute | solution.py:527
  178.1 0.7 copy-done.14
  178.9 3.9 %join.5 = (f32[16,96,128]{2,1,0:T(8,128)}, f32[16,96,128]{2,1,0:T(8,128)}, bf16[16,96,128]{2,1,0:T(8,128)(2,1)}) custom-call(f32[16,96,128]{2,1,0:T(8,128)} %get-tuple-element.23.chip_ref, f32[16,96,128]{2,1,0:T(8,128)} %get-tuple-element.24.before_ref, bf16[16,96,128]{2,1,0:T(8,128)(2,1)} %copy-done.14, ...), custom_call_target="tpu_custom_call" | custom-call | flops 1000 | bytes 1000 | tf_op jit(solution)/shard_map/join/pallas_call | solution.py:377
  182.8 1.4 copy-done.2
  184.2 1.3 collective-permute-start.12
  185.5 2.4 pack.6.rest_0_
  187.9 0.7 copy-done.17
  188.6 16.9 %mix_final.1.rest_0_ = bf16[512,3072]{1,0:T(8,128)(2,1)} custom-call(s32[1]{0:T(128)} %bitcast.info, bf16[512,3072]{1,0:T(8,128)(2,1)} %query_ref.8, f32[512,3072]{1,0:T(8,128)} %mix_local.1.rest_0_.local_ref, f32[8,512,4]{2,1,0:T(8,128)} %bitcast.21, f32[16,96,128]{2,1,0:T(8,128)} %get-tuple-element.26.own_ref, bf16[16,96,128]{2,1,0:T(8,128)(2,1)} %copy-done.17, ...), custom_call_target="tpu_custom_call" | custom-call | flops 1000 | bytes 1000 | tf_op jit(solution)/shard_map/mix_final/pallas_call | solution.py:490
  205.6 15.9 %convolution_convert_fusion.rest_0_.refs_1_ = bf16[512,3072]{1,0:T(8,128)(2,1)} fusion(bf16[512,3072]{1,0:T(8,128)(2,1)} %mix_final.1.rest_0_, bf16[3072,3072]{1,0:T(8,128)(2,1)} %param.12), kind=kOutput, calls=%fused_computation | convolution fusion | flops 9665249280 | bytes 25165824 | tf_op jit(solution)/shard_map/dot_general | solution.py:614
  221.5 1.4 copy-done.6
  222.9 1.3 collective-permute-start.17
  224.2 4.3 %pick.5.mid_ref = bf16[2,512,1152]{2,1,0:T(8,128)(2,1)} custom-call(s32[1]{0:T(128)} %bitcast.info, bf16[2,512,1152]{2,1,0:T(8,128)(2,1)} %collective-permute-done.8.rest_1_.chip_ref, bf16[2,512,1152]{2,1,0:T(8,128)(2,1)} %collective-permute-done.12.back_ref, bf16[512,3072]{1,0:T(8,128)(2,1)} %mix_final.1.rest_0_), custom_call_target="tpu_custom_call" | custom-call | flops 1000 | bytes 1000 | tf_op jit(solution)/shard_map/pick/pallas_call | solution.py:99
  228.5 1.9 collective-permute-start.13
  230.4 5.7 %collective-permute-start.16 = (bf16[2,512,768]{2,1,0:T(8,128)(2,1)S(1)}, bf16[2,512,768]{2,1,0:T(8,128)(2,1)}, u32[]{:S(2)}, u32[]{:S(2)}) collective-permute-start(bf16[2,512,768]{2,1,0:T(8,128)(2,1)S(1)} %copy-done.6), channel_id=1, source_target_pairs={{0,4},{2,6},{4,8},{8,12},{10,14},{12,16},{16,20},{18,22},{20,24},{... | collective-permute-start | bytes 4718600 | tf_op jit(solution)/shard_map/ppermute | solution.py:527
  236.1 1.1 copy-done.5
  237.3 1.3 collective-permute-start.18
  238.6 2.1 pack.7.rest_1_
  240.7 1.3 collective-permute-start.10
  242.0 1.3 collective-permute-start.14
  243.3 20.4 %attend.5.refs_1_.rest_0_ = bf16[512,3072]{1,0:T(8,128)(2,1)} custom-call(s32[1]{0:T(128)} %bitcast.info, bf16[512,3072]{1,0:T(8,128)(2,1)} %query_ref.11, bf16[512,3072]{1,0:T(8,128)(2,1)} %key_ref.19, bf16[512,3072]{1,0:T(8,128)(2,1)} %value_ref.19, bf16[2,512,1152]{2,1,0:T(8,128)(2,1)} %gate.5.near_ref, ...), custom_call_target="tpu_custom_call", output_to_operand_aliasing={{}: (7, {})} | custom-call | flops 1000 | bytes 1000 | tf_op jit(solution)/shard_map/attend/pallas_call | solution.py:217
  263.7 5.0 %collective-permute-done.16.chip_ref = bf16[2,512,768]{2,1,0:T(8,128)(2,1)} collective-permute-done((bf16[2,512,768]{2,1,0:T(8,128)(2,1)S(1)}, bf16[2,512,768]{2,1,0:T(8,128)(2,1)}, u32[]{:S(2)}, u32[]{:S(2)}) %collective-permute-start.16) | collective-permute-done | bytes 1572896 | tf_op jit(solution)/shard_map/ppermute | solution.py:527
  268.7 21.1 %collective-permute-done.18.back_ref = bf16[2,512,768]{2,1,0:T(8,128)(2,1)} collective-permute-done((bf16[2,512,768]{2,1,0:T(8,128)(2,1)}, bf16[2,512,768]{2,1,0:T(8,128)(2,1)}, u32[]{:S(2)}, u32[]{:S(2)}) %collective-permute-start.18) | collective-permute-done | bytes 1572896 | tf_op jit(solution)/shard_map/ppermute | solution.py:527
  289.8 2.9 pick.6.rest_0_.mid_ref
  292.7 0.9 copy-done.7
  293.6 1.3 collective-permute-start.15
  294.9 12.2 %collective-permute-done.15.back_ref = bf16[2,512,384]{2,1,0:T(8,128)(2,1)S(1)} collective-permute-done((bf16[2,512,384]{2,1,0:T(8,128)(2,1)}, bf16[2,512,384]{2,1,0:T(8,128)(2,1)S(1)}, u32[]{:S(2)}, u32[]{:S(2)}) %collective-permute-start.15) | collective-permute-done | bytes 786464 | tf_op jit(solution)/shard_map/ppermute | solution.py:527
  307.1 0.9 copy-done.12
  308.0 2.3 pick.7.rest_1_.mid_ref
  310.3 1.2 copy-done.9
  311.5 14.7 %attend.6.rest_1_ = bf16[512,3072]{1,0:T(8,128)(2,1)} custom-call(s32[1]{0:T(128)} %bitcast.info, bf16[512,3072]{1,0:T(8,128)(2,1)} %query_ref.11, bf16[512,3072]{1,0:T(8,128)(2,1)} %key_ref.19, bf16[512,3072]{1,0:T(8,128)(2,1)} %value_ref.19, bf16[2,512,768]{2,1,0:T(8,128)(2,1)} %gate.7.near_ref, ...), custom_call_target="tpu_custom_call", output_to_operand_aliasing={{}: (7, {})} | custom-call | flops 1000 | bytes 1000 | tf_op jit(solution)/shard_map/attend/pallas_call | solution.py:217
  326.3 3.8 %copy.33.rest_0_ = bf16[512,3072]{1,0:T(8,128)(2,1)} copy(bf16[512,3072]{1,0:T(8,128)(2,1)} %attend.6.rest_1_) | data formatting | bytes 6291456
  330.0 0.9 copy-done.10
  330.9 8.5 %attend.7 = bf16[512,3072]{1,0:T(8,128)(2,1)} custom-call(s32[1]{0:T(128)} %bitcast.info, bf16[512,3072]{1,0:T(8,128)(2,1)} %query_ref.11, bf16[512,3072]{1,0:T(8,128)(2,1)} %key_ref.19, bf16[512,3072]{1,0:T(8,128)(2,1)} %value_ref.19, bf16[2,512,384]{2,1,0:T(8,128)(2,1)} %gate.6.near_ref, ...), custom_call_target="tpu_custom_call", output_to_operand_aliasing={{}: (7, {})} | custom-call | flops 1000 | bytes 1000 | tf_op jit(solution)/shard_map/attend/pallas_call | solution.py:217
  (53 shorter events, 0.3 us)
Async XLA Ops:
  7.2 6.9 %copy-start = (f32[512,32]{0,1:T(8,128)S(1)}, f32[512,32]{0,1:T(8,128)}, u32[]{:S(2)}) copy-start(f32[512,32]{0,1:T(8,128)} %param.11) | copy-start | bytes 196612
  7.2 332.2 %reduce-scatter.2.cloned.1.call-start = ((), (), s32[]{:S(2)}) async-start(), calls=%async_computation.1 | async-start | bytes 4718592 | tf_op jit(solution)/shard_map/reduce_scatter | solution.py:616
  9.6 24.2 %collective-permute-start.3 = (bf16[2,512,768]{2,1,0:T(8,128)(2,1)}, bf16[2,512,768]{2,1,0:T(8,128)(2,1)S(1)}, u32[]{:S(2)}, u32[]{:S(2)}) collective-permute-start(bf16[2,512,768]{2,1,0:T(8,128)(2,1)} %pack.4.rest_0_), channel_id=1, source_target_pairs={{0,2},{2,8},{4,6},{6,12},{8,10},{10,16},{12,14},{14,20},{16,18},{1... | collective-permute-start | bytes 4718600 | tf_op jit(solution)/shard_map/ppermute | solution.py:527
  10.9 58.6 %collective-permute-start.1 = (bf16[2,512,768]{2,1,0:T(8,128)(2,1)}, bf16[2,512,768]{2,1,0:T(8,128)(2,1)S(1)}, u32[]{:S(2)}, u32[]{:S(2)}) collective-permute-start(bf16[2,512,768]{2,1,0:T(8,128)(2,1)} %pack.4.rest_0_), channel_id=1, source_target_pairs={{0,4},{2,6},{4,8},{8,12},{10,14},{12,16},{16,20},{18,22},{20,24},{... | collective-permute-start | bytes 4718600 | tf_op jit(solution)/shard_map/ppermute | solution.py:527
  33.7 1.1 copy-start.4
  34.9 58.9 %collective-permute-start.4 = (bf16[2,512,768]{2,1,0:T(8,128)(2,1)}, bf16[2,512,768]{2,1,0:T(8,128)(2,1)}, u32[]{:S(2)}, u32[]{:S(2)}) collective-permute-start(bf16[2,512,768]{2,1,0:T(8,128)(2,1)} %gate.4.near_ref), channel_id=1, source_target_pairs={{12,10},{20,18},{28,26},{13,11},{21,19},{29,27}} | collective-permute-start | bytes 4718600 | tf_op jit(solution)/shard_map/ppermute | solution.py:527
  36.1 33.3 %collective-permute-start = (bf16[32,96,128]{2,1,0:T(8,128)(2,1)}, bf16[32,96,128]{2,1,0:T(8,128)(2,1)S(1)}, u32[]{:S(2)}, u32[]{:S(2)}) collective-permute-start(bf16[32,96,128]{2,1,0:T(8,128)(2,1)} %get-tuple-element.16.rest_0_), channel_id=1, source_target_pairs={{0,2},{2,0},{4,6},{6,4},{8,10},{10,8},{12,14},{14,12},{16,18},{18,... | collective-permute-start | bytes 2359304 | tf_op jit(solution)/shard_map/ppermute | solution.py:527
  38.2 127.4 %collective-permute-start.8 = (bf16[2,512,1152]{2,1,0:T(8,128)(2,1)}, bf16[2,512,1152]{2,1,0:T(8,128)(2,1)}, u32[]{:S(2)}, u32[]{:S(2)}) collective-permute-start(bf16[2,512,1152]{2,1,0:T(8,128)(2,1)} %pack.5.rest_0_.refs_1_), channel_id=1, source_target_pairs={{0,4},{2,6},{4,8},{8,12},{10,14},{12,16},{16,20},{18,22},{20,24},{... | collective-permute-start | bytes 7077896 | tf_op jit(solution)/shard_map/ppermute | solution.py:527
  69.4 0.9 copy-start.8
  69.4 1.4 copy-start.3
  93.7 4.0 %copy-start.16 = (bf16[16,96,128]{2,1,0:T(8,128)(2,1)S(1)}, bf16[16,96,128]{2,1,0:T(8,128)(2,1)}, u32[]{:S(2)}) copy-start(bf16[16,96,128]{2,1,0:T(8,128)(2,1)} %get-tuple-element.19.rest_0_) | copy-start | bytes 1179652
  96.5 48.1 %collective-permute-start.6 = (bf16[2,512,768]{2,1,0:T(8,128)(2,1)}, bf16[2,512,768]{2,1,0:T(8,128)(2,1)}, u32[]{:S(2)}, u32[]{:S(2)}) collective-permute-start(bf16[2,512,768]{2,1,0:T(8,128)(2,1)} %pick.4.rest_0_.mid_ref), channel_id=1, source_target_pairs={{0,2},{2,0},{4,6},{6,4},{8,10},{10,8},{12,14},{14,12},{16,18},{18,... | collective-permute-start | bytes 4718600 | tf_op jit(solution)/shard_map/ppermute | solution.py:527
  96.5 86.4 %collective-permute-start.11 = (bf16[2,512,1152]{2,1,0:T(8,128)(2,1)}, bf16[2,512,1152]{2,1,0:T(8,128)(2,1)S(1)}, u32[]{:S(2)}, u32[]{:S(2)}) collective-permute-start(bf16[2,512,1152]{2,1,0:T(8,128)(2,1)} %pack.5.rest_0_.refs_1_), channel_id=1, source_target_pairs={{0,2},{2,8},{4,6},{6,12},{8,10},{10,16},{12,14},{14,20},{16,18},{1... | collective-permute-start | bytes 7077896 | tf_op jit(solution)/shard_map/ppermute | solution.py:527
  97.8 40.7 %collective-permute-start.2 = (bf16[16,96,128]{2,1,0:T(8,128)(2,1)S(1)}, bf16[16,96,128]{2,1,0:T(8,128)(2,1)S(1)}, u32[]{:S(2)}, u32[]{:S(2)}) collective-permute-start(bf16[16,96,128]{2,1,0:T(8,128)(2,1)S(1)} %copy-done.16), channel_id=1, source_target_pairs={{0,4},{2,6},{4,8},{6,10},{8,12},{10,14},{12,16},{14,18},{16,20},{1... | collective-permute-start | bytes 1179656 | tf_op jit(solution)/shard_map/ppermute | solution.py:527
  138.5 0.8 copy-start.15
  143.1 16.0 %collective-permute-start.5 = (bf16[16,96,128]{2,1,0:T(8,128)(2,1)}, bf16[16,96,128]{2,1,0:T(8,128)(2,1)S(1)}, u32[]{:S(2)}, u32[]{:S(2)}) collective-permute-start(bf16[16,96,128]{2,1,0:T(8,128)(2,1)} %get-tuple-element.22.rest_0_), channel_id=1, source_target_pairs={{0,8},{2,10},{4,12},{6,14},{8,16},{10,18},{12,20},{14,22},{16,24},... | collective-permute-start | bytes 1179656 | tf_op jit(solution)/shard_map/ppermute | solution.py:527
  159.1 0.7 copy-start.13
  164.3 13.8 %collective-permute-start.7 = (bf16[16,96,128]{2,1,0:T(8,128)(2,1)}, bf16[16,96,128]{2,1,0:T(8,128)(2,1)S(1)}, u32[]{:S(2)}, u32[]{:S(2)}) collective-permute-start(bf16[16,96,128]{2,1,0:T(8,128)(2,1)} %get-tuple-element.25.rest_0_.refs_1_), channel_id=1, source_target_pairs={{0,16},{2,18},{4,20},{6,22},{8,24},{10,26},{12,28},{14,30},{1,17},... | collective-permute-start | bytes 1179656 | tf_op jit(solution)/shard_map/ppermute | solution.py:527
  178.1 0.7 copy-start.14
  182.8 5.1 %collective-permute-start.9 = (bf16[16,96,128]{2,1,0:T(8,128)(2,1)}, bf16[16,96,128]{2,1,0:T(8,128)(2,1)S(1)}, u32[]{:S(2)}, u32[]{:S(2)}) collective-permute-start(bf16[16,96,128]{2,1,0:T(8,128)(2,1)} %get-tuple-element.27.rest_0_), channel_id=1, source_target_pairs={{0,2},{2,0},{4,6},{6,4},{8,10},{10,8},{12,14},{14,12},{16,18},{18,... | collective-permute-start | bytes 1179656 | tf_op jit(solution)/shard_map/ppermute | solution.py:527
  182.8 1.4 copy-start.2
  184.2 40.0 %collective-permute-start.12 = (bf16[2,512,1152]{2,1,0:T(8,128)(2,1)}, bf16[2,512,1152]{2,1,0:T(8,128)(2,1)}, u32[]{:S(2)}, u32[]{:S(2)}) collective-permute-start(bf16[2,512,1152]{2,1,0:T(8,128)(2,1)} %gate.5.near_ref), channel_id=1, source_target_pairs={{12,10},{20,18},{28,26},{13,11},{21,19},{29,27}} | collective-permute-start | bytes 7077896 | tf_op jit(solution)/shard_map/ppermute | solution.py:527
  187.9 0.7 copy-start.17
  221.5 1.4 copy-start.6
  222.9 13.2 %collective-permute-start.17 = (bf16[2,512,768]{2,1,0:T(8,128)(2,1)S(1)}, bf16[2,512,768]{2,1,0:T(8,128)(2,1)S(1)}, u32[]{:S(2)}, u32[]{:S(2)}) collective-permute-start(bf16[2,512,768]{2,1,0:T(8,128)(2,1)S(1)} %copy-done.6), channel_id=1, source_target_pairs={{0,2},{2,8},{4,6},{6,12},{8,10},{10,16},{12,14},{14,20},{16,18},{1... | collective-permute-start | bytes 4718600 | tf_op jit(solution)/shard_map/ppermute | solution.py:527
  228.5 14.8 %collective-permute-start.13 = (bf16[2,512,1152]{2,1,0:T(8,128)(2,1)}, bf16[2,512,1152]{2,1,0:T(8,128)(2,1)}, u32[]{:S(2)}, u32[]{:S(2)}) collective-permute-start(bf16[2,512,1152]{2,1,0:T(8,128)(2,1)} %pick.5.mid_ref), channel_id=1, source_target_pairs={{0,2},{2,0},{4,6},{6,4},{8,10},{10,8},{12,14},{14,12},{16,18},{18,... | collective-permute-start | bytes 7077896 | tf_op jit(solution)/shard_map/ppermute | solution.py:527
  230.4 38.3 %collective-permute-start.16 = (bf16[2,512,768]{2,1,0:T(8,128)(2,1)S(1)}, bf16[2,512,768]{2,1,0:T(8,128)(2,1)}, u32[]{:S(2)}, u32[]{:S(2)}) collective-permute-start(bf16[2,512,768]{2,1,0:T(8,128)(2,1)S(1)} %copy-done.6), channel_id=1, source_target_pairs={{0,4},{2,6},{4,8},{8,12},{10,14},{12,16},{16,20},{18,22},{20,24},{... | collective-permute-start | bytes 4718600 | tf_op jit(solution)/shard_map/ppermute | solution.py:527
  236.1 1.1 copy-start.5
  237.3 52.5 %collective-permute-start.18 = (bf16[2,512,768]{2,1,0:T(8,128)(2,1)}, bf16[2,512,768]{2,1,0:T(8,128)(2,1)}, u32[]{:S(2)}, u32[]{:S(2)}) collective-permute-start(bf16[2,512,768]{2,1,0:T(8,128)(2,1)} %gate.7.near_ref), channel_id=1, source_target_pairs={{12,10},{20,18},{28,26},{13,11},{21,19},{29,27}} | collective-permute-start | bytes 4718600 | tf_op jit(solution)/shard_map/ppermute | solution.py:527
  240.7 52.0 %collective-permute-start.10 = (bf16[2,512,384]{2,1,0:T(8,128)(2,1)}, bf16[2,512,384]{2,1,0:T(8,128)(2,1)S(1)}, u32[]{:S(2)}, u32[]{:S(2)}) collective-permute-start(bf16[2,512,384]{2,1,0:T(8,128)(2,1)} %pack.7.rest_1_), channel_id=1, source_target_pairs={{0,2},{2,8},{4,6},{6,12},{8,10},{10,16},{12,14},{14,20},{16,18},{1... | collective-permute-start | bytes 2359304 | tf_op jit(solution)/shard_map/ppermute | solution.py:527
  242.0 52.9 %collective-permute-start.14 = (bf16[2,512,384]{2,1,0:T(8,128)(2,1)}, bf16[2,512,384]{2,1,0:T(8,128)(2,1)S(1)}, u32[]{:S(2)}, u32[]{:S(2)}) collective-permute-start(bf16[2,512,384]{2,1,0:T(8,128)(2,1)} %pack.7.rest_1_), channel_id=1, source_target_pairs={{0,4},{2,6},{4,8},{8,12},{10,14},{12,16},{16,20},{18,22},{20,24},{... | collective-permute-start | bytes 2359304 | tf_op jit(solution)/shard_map/ppermute | solution.py:527
  292.7 17.6 %collective-permute-start.20 = (bf16[2,512,768]{2,1,0:T(8,128)(2,1)}, bf16[2,512,768]{2,1,0:T(8,128)(2,1)S(1)}, u32[]{:S(2)}, u32[]{:S(2)}) collective-permute-start(bf16[2,512,768]{2,1,0:T(8,128)(2,1)} %pick.6.rest_0_.mid_ref), channel_id=1, source_target_pairs={{0,2},{2,0},{4,6},{6,4},{8,10},{10,8},{12,14},{14,12},{16,18},{18,... | collective-permute-start | bytes 4718600 | tf_op jit(solution)/shard_map/ppermute | solution.py:527
  292.7 0.9 copy-start.7
  293.6 13.5 %collective-permute-start.15 = (bf16[2,512,384]{2,1,0:T(8,128)(2,1)}, bf16[2,512,384]{2,1,0:T(8,128)(2,1)S(1)}, u32[]{:S(2)}, u32[]{:S(2)}) collective-permute-start(bf16[2,512,384]{2,1,0:T(8,128)(2,1)} %gate.6.near_ref), channel_id=1, source_target_pairs={{12,10},{20,18},{28,26},{13,11},{21,19},{29,27}} | collective-permute-start | bytes 2359304 | tf_op jit(solution)/shard_map/ppermute | solution.py:527
  294.9 12.2 %copy-start.11 = (bf16[2,512,384]{2,1,0:T(8,128)(2,1)}, bf16[2,512,384]{2,1,0:T(8,128)(2,1)S(1)}, u32[]{:S(2)}) copy-start(bf16[2,512,384]{2,1,0:T(8,128)(2,1)S(1)} %collective-permute-done.14.chip_ref) | copy-start | bytes 2359300
  307.1 0.9 copy-start.12
  310.3 19.7 %collective-permute-start.19 = (bf16[2,512,384]{2,1,0:T(8,128)(2,1)}, bf16[2,512,384]{2,1,0:T(8,128)(2,1)S(1)}, u32[]{:S(2)}, u32[]{:S(2)}) collective-permute-start(bf16[2,512,384]{2,1,0:T(8,128)(2,1)} %pick.7.rest_1_.mid_ref), channel_id=1, source_target_pairs={{0,2},{2,0},{4,6},{6,4},{8,10},{10,8},{12,14},{14,12},{16,18},{18,... | collective-permute-start | bytes 2359304 | tf_op jit(solution)/shard_map/ppermute | solution.py:527
  310.3 1.2 copy-start.9
  330.0 0.9 copy-start.10
  330.9 8.5 %copy-start.1 = (f32[512,32]{0,1:T(8,128)S(1)}, f32[512,32]{0,1:T(8,128)}, u32[]{:S(2)}) copy-start(f32[512,32]{0,1:T(8,128)} %param.11) | copy-start | bytes 196612
Sparse Core Ops, SparseCore 0:
  221.6 46.2 reduce-scatter.1
where the time goes:
time: 352 us; the launch traced here: 347 us
  Pallas kernels  140 us (40%)
  waiting for transfers between devices  109 us (31%)
  starting transfers between devices  45.7 us (13%)
  local copies, waits for them, and re-layouts  19.9 us (6%)
  matrix products  15.9 us (5%)
  between operations  14.6 us (4%)
    ppermute x21, waiting for transfers between devices, moved(): lax.ppermute(value, 'ctx', [(s, t) for s, t in pairs if 0 <= t < count])  109 us
    pallas_call x4, Pallas kernels, attend(): pl.pallas_call(attend_kernel, grid_spec=pltpu.PrefetchScalarGridSpec(num_...  58.2 us
    ppermute x21, starting transfers between devices, moved(): lax.ppermute(value, 'ctx', [(s, t) for s, t in pairs if 0 <= t < count])  45.7 us
    unnamed x37, local copies, waits for them, and re-layouts  17 us
    pallas_call x1, Pallas kernels, mix_final(): pl.pallas_call(functools.partial(mix_final_kernel, half), grid_spec=pltpu...  16.9 us
    dot_general x1, matrix products, do_project(): jnp.dot(light['normed'], out_weight, preferred_element_type=jnp.float32)  15.9 us
    pallas_call x1, Pallas kernels, mix_local(): pl.pallas_call(mix_local_kernel, grid=(width // WIDE,), in_specs=[block,...  13.9 us
    pallas_call x3, Pallas kernels, join(): pl.pallas_call(functools.partial(join_kernel, start, last), grid=(chip.sh...  12.3 us
  transfers between devices with their start and end apart: 22, of which 6 were waited for; matrix products, arithmetic and copies ran while one was open for 7% of the time, Pallas kernels for 40%

commit v1 on v0

--- a/solution.py
+++ b/solution.py
@@ -14,7 +14,7 @@
 WIDE = BUNDLE * DH
 LANES = 128
 EPS_NORM = 1e-06
-VMEM_BYTES = 60 * 1024 * 1024
+VMEM_BYTES = 63 * 1024 * 1024
 WINDOWS = ((0, 128, 0), (0, 256, 96), (128, 256, 64), (256, 128, 32))
 
 
@@ -27,7 +27,7 @@
 
 
 def untouched(deps):
-    return [pl.BlockSpec(memory_space=pltpu.HBM)] * len(deps)
+    return [pl.BlockSpec(memory_space=pl.ANY)] * len(deps)
 
 
 def gate_kernel(*refs):
@@ -38,7 +38,7 @@
     return pl.pallas_call(
         gate_kernel,
         in_specs=untouched([value, *deps]),
-        out_specs=pl.BlockSpec(memory_space=pltpu.HBM),
+        out_specs=pl.BlockSpec(memory_space=pl.ANY),
         out_shape=jax.ShapeDtypeStruct(value.shape, value.dtype),
         input_output_aliases={0: 0},
         compiler_params=params(),
@@ -52,21 +52,27 @@
     return (lane >= start) & (lane < start + DH)
 
 
-def pack_kernel(key_ref, value_ref, *rest):
-    out_ref = rest[-1]
-    out_ref[0] = key_ref[...]
-    out_ref[1] = value_ref[...]
+def pack_kernel(base, key_ref, value_ref, *rest):
+    out_ref, sems = rest[-2:]
+    width = out_ref.shape[2]
+    copies = [
+        pltpu.make_async_copy(ref.at[:, pl.ds(base * WIDE, width)], out_ref.at[i], sems.at[i])
+        for i, ref in enumerate((key_ref, value_ref))
+    ]
+    for copy in copies:
+        copy.start()
+    for copy in copies:
+        copy.wait()
 
 
 def pack(key, value, base, bundles, deps):
     rows = key.shape[0]
-    block = pl.BlockSpec((rows, WIDE), lambda b: (0, base + b))
-    return pl.pallas_call(
-        pack_kernel,
-        grid=(bundles,),
-        in_specs=[block, block] + untouched(deps),
-        out_specs=pl.BlockSpec((2, rows, WIDE), lambda b: (0, 0, b)),
+    return pl.pallas_call(
+        functools.partial(pack_kernel, base),
+        in_specs=untouched([key, value, *deps]),
+        out_specs=pl.BlockSpec(memory_space=pl.ANY),
         out_shape=jax.ShapeDtypeStruct((2, rows, bundles * WIDE), key.dtype),
+        scratch_shapes=[pltpu.SemaphoreType.DMA((2,))],
         compiler_params=params(),
         cost_estimate=cheap(),
         name="pack",
@@ -74,38 +80,29 @@
 
 
 def pick_kernel(info, chip_ref, back_ref, *rest):
-    out_ref = rest[-1]
+    out_ref, sem = rest[-2:]
     from_back = lax.rem(info[0], 4) == 1
 
     @pl.when(from_back)
     def _():
-        out_ref[...] = back_ref[...]
+        copy = pltpu.make_async_copy(back_ref, out_ref, sem)
+        copy.start()
+        copy.wait()
 
     @pl.when(jnp.logical_not(from_back))
     def _():
-        out_ref[...] = chip_ref[...]
+        copy = pltpu.make_async_copy(chip_ref, out_ref, sem)
+        copy.start()
+        copy.wait()
 
 
 def pick(info, chip, back, deps):
-    _, rows, width = chip.shape
-    shape = (2, rows, WIDE)
-
-    def from_chip(b, info):
-        return (0, 0, jnp.where(lax.rem(info[0], 4) == 1, 0, b))
-
-    def from_back(b, info):
-        return (0, 0, jnp.where(lax.rem(info[0], 4) == 1, b, 0))
-
     return pl.pallas_call(
         pick_kernel,
-        grid_spec=pltpu.PrefetchScalarGridSpec(
-            num_scalar_prefetch=1,
-            grid=(width // WIDE,),
-            in_specs=[pl.BlockSpec(shape, from_chip), pl.BlockSpec(shape, from_back)]
-            + untouched(deps),
-            out_specs=pl.BlockSpec(shape, lambda b, _: (0, 0, b)),
-        ),
+        in_specs=[pl.BlockSpec(memory_space=pltpu.SMEM)] + untouched([chip, back, *deps]),
+        out_specs=pl.BlockSpec(memory_space=pl.ANY),
         out_shape=jax.ShapeDtypeStruct(chip.shape, chip.dtype),
+        scratch_shapes=[pltpu.SemaphoreType.DMA],
         compiler_params=params(),
         cost_estimate=cheap(),
         name="pick",
@@ -192,6 +189,61 @@
         ready = following
 
 
+def attend_bounded(exists, query_ref, slots, out_ref):
+    rows = query_ref.shape[0]
+    scale = jnp.float32(math.log2(math.e) / math.sqrt(DH))
+    row = lax.broadcasted_iota(jnp.int32, (SUB, SUB), 0)
+    col = lax.broadcasted_iota(jnp.int32, (SUB, SUB), 1)
+    newer, older = col > row, col <= row
+    low = jnp.float32(-1e30)
+    for part in range(rows // SUB):
+        first = part * SUB
+        spans = [(first, rows), (0, rows), (0, rows), (0, first + SUB)]
+        tiles_out = [None] * (WIDE // LANES)
+        for start, width, place in WINDOWS:
+            lanes = slice(start, start + width)
+            query = query_ref[first : first + SUB, lanes]
+            query = jnp.where(head_lanes(query.shape, place), query, jnp.zeros_like(query))
+            result = None
+            for slot in range(4):
+                begin, end = spans[slot]
+                weights = []
+                for at in range(begin, end, SUB):
+                    score = lax.dot_general(
+                        query,
+                        slots[slot][0][at : at + SUB, lanes],
+                        (((1,), (1,)), ((), ())),
+                        preferred_element_type=jnp.float32,
+                    )
+                    if slot == 0 and at == begin:
+                        score = jnp.where(newer, score, low)
+                    if slot == 3 and at == end - SUB:
+                        score = jnp.where(older, score, low)
+                    weights.append(jnp.exp2(score * scale).astype(jnp.bfloat16))
+                weight = weights[0] if len(weights) == 1 else jnp.concatenate(weights, axis=1)
+                value = slots[slot][1][begin:end, lanes]
+                one = jnp.ones_like(value)
+                if slot < 3:
+                    one = jnp.full(value.shape, exists[slot].astype(jnp.float32), value.dtype)
+                value = jnp.where(head_lanes(value.shape, place), value, one)
+                term = jnp.dot(weight, value, preferred_element_type=jnp.float32)
+                result = term if result is None else result + term
+            spare = 96 if place == 0 else 0
+            result = result * (1.0 / result[:, spare : spare + 1])
+            spread(jnp.where(head_lanes(result.shape, place), result, 0.0), start, tiles_out)
+        for tile, piece in enumerate(tiles_out):
+            out_ref[first : first + SUB, tile * LANES : (tile + 1) * LANES] = piece.astype(
+                out_ref.dtype
+            )
+
+
+def spread(result, start, tiles_out):
+    for lane in range(0, result.shape[1], LANES):
+        tile = (start + lane) // LANES
+        piece = result[:, lane : lane + LANES]
+        tiles_out[tile] = piece if tiles_out[tile] is None else tiles_out[tile] + piece
+
+
 def attend_kernel(info, query_ref, key_ref, value_ref, near_ref, mid_ref, swap_ref, *rest):
     out_ref = rest[-1]
     position = info[0]
@@ -199,14 +251,25 @@
     own = (key_ref, value_ref)
     near, mid, swap = [(r.at[0], r.at[1]) for r in (near_ref, mid_ref, swap_ref)]
     core = lax.rem(position, 2)
-
-    @pl.when(core == 0)
-    def _():
-        attend_body(exists, query_ref, [near, mid, swap, own], out_ref)
-
-    @pl.when(core == 1)
-    def _():
-        attend_body(exists, query_ref, [swap, mid, near, own], out_ref)
+    sums = jnp.abs(query_ref[...].astype(jnp.float32))
+    most = None
+    for start, width, place in WINDOWS:
+        part = sums[:, start : start + width]
+        part = jnp.sum(jnp.where(head_lanes(part.shape, place), part, 0.0), axis=1, keepdims=True)
+        most = part if most is None else jnp.maximum(most, part)
+    top = None
+    for key, _ in (near, mid, swap, own):
+        one = jnp.max(jnp.abs(key[...]), axis=0, keepdims=True)
+        top = one if top is None else jnp.maximum(top, one)
+    limit = 100.0 * math.sqrt(DH) / math.log2(math.e)
+    bounded = jnp.max(most) * jnp.max(top.astype(jnp.float32)) < limit
+
+    for side in range(2):
+        for body, chosen in ((attend_bounded, bounded), (attend_body, jnp.logical_not(bounded))):
+            @pl.when((core == side) & chosen)
+            def _(body=body, side=side):
+                old, new = (near, swap) if side == 0 else (swap, near)
+                body(exists, query_ref, [old, mid, new, own], out_ref)
 
 
 def attend(info, query, key, value, near, mid, swap, out, base, deps):
@@ -258,12 +321,12 @@
         lanes = slice(start, start + width)
         state, before = None, None
         for at in range(0, rows, SUB):
-            running = decay_ref[0, at : at + SUB, head : head + 1]
-            anchor = running[SUB - 1 :, :]
-            value = value_ref[at : at + SUB, lanes].astype(jnp.float32) * jnp.exp(anchor - running)
+            running = decay_ref[0, head : head + 1, at : at + SUB]
+            anchor = running[:, SUB - 1 :]
+            key = key_t[head * DH : (head + 1) * DH, at : at + SUB].astype(jnp.float32)
             update = jnp.dot(
-                key_t[head * DH : (head + 1) * DH, at : at + SUB],
-                value.astype(jnp.bfloat16),
+                (key * jnp.exp(anchor - running)).astype(jnp.bfloat16),
+                value_ref[at : at + SUB, lanes],
                 preferred_element_type=jnp.float32,
             )
             if at + SUB == rows:
@@ -300,7 +363,7 @@
     return jnp.concatenate(pads, axis=0).astype(jnp.bfloat16)
 
 
-def local_state(key, value, decay_cols, deps):
+def local_state(key, value, decay_rows, deps):
     rows, width = key.shape
     bundles = width // WIDE
     block = pl.BlockSpec((rows, WIDE), lambda b: (0, b))
@@ -309,7 +372,7 @@
     return pl.pallas_call(
         state_kernel,
         grid=(bundles,),
-        in_specs=[block, block, pl.BlockSpec((1, rows, BUNDLE), lambda b: (b, 0, 0))]
+        in_specs=[block, block, pl.BlockSpec((1, BUNDLE, rows), lambda b: (b, 0, 0))]
         + untouched(deps),
         out_specs=[out, out, out],
         out_shape=[
@@ -320,7 +383,7 @@
         compiler_params=params(),
         cost_estimate=cheap(),
         name="local_state",
-    )(key, value, decay_cols, *deps)
+    )(key, value, decay_rows, *deps)
 
 
 def chip_state_kernel(info, exact_ref, other_ref, *rest):
@@ -335,18 +398,17 @@
 def chip_state(info, exact, other, deps):
     half = exact.shape[0] // 2
     shape = (half, DH, LANES)
-    block = pl.BlockSpec((BUNDLE, DH, LANES), lambda b, _: (b, 0, 0))
-    steps = half // BUNDLE
+    block = pl.BlockSpec(shape, lambda b, _: (0, 0, 0))
 
     def mine(b, info):
-        return (lax.rem(info[0], 2) * steps + b, 0, 0)
+        return (lax.rem(info[0], 2), 0, 0)
 
     return pl.pallas_call(
         chip_state_kernel,
         grid_spec=pltpu.PrefetchScalarGridSpec(
             num_scalar_prefetch=1,
-            grid=(steps,),
-            in_specs=[pl.BlockSpec((BUNDLE, DH, LANES), mine)] * 2 + untouched(deps),
+            grid=(1,),
+            in_specs=[pl.BlockSpec(shape, mine)] * 2 + untouched(deps),
             out_specs=[block, block],
         ),
         out_shape=[
@@ -373,10 +435,10 @@
 
 
 def join(chip, before, arrived, start, last, deps):
-    block = pl.BlockSpec((BUNDLE, DH, LANES), lambda b: (b, 0, 0))
+    block = pl.BlockSpec(chip.shape, lambda b: (0, 0, 0))
     return pl.pallas_call(
         functools.partial(join_kernel, start, last),
-        grid=(chip.shape[0] // BUNDLE,),
+        grid=(1,),
         in_specs=[block] * 3 + untouched(deps),
         out_specs=[block] * 3,
         out_shape=[
@@ -388,13 +450,6 @@
         cost_estimate=cheap(),
         name="join",
     )(chip, before, arrived, *deps)
-
-
-def spread(result, start, tiles_out):
-    for lane in range(0, result.shape[1], LANES):
-        tile = (start + lane) // LANES
-        piece = result[:, lane : lane + LANES]
-        tiles_out[tile] = piece if tiles_out[tile] is None else tiles_out[tile] + piece
 
 
 def mix_local_kernel(query_ref, key_ref, value_ref, col_ref, row_ref, first_ref, *rest):
@@ -475,7 +530,8 @@
             result = jnp.dot(scaled, states[head], preferred_element_type=jnp.float32)
             result = jnp.where(inside, result + local_ref[here, lanes], 0.0)
             square = jnp.sum(result * result, axis=1, keepdims=True) * (1.0 / DH)
-            spread(result * lax.rsqrt(square + EPS_NORM), start, tiles_out)
+            factor = lax.rsqrt(square + EPS_NORM)
+            spread(result * factor, start, tiles_out)
         for tile, piece in enumerate(tiles_out):
             out_ref[here, tile * LANES : (tile + 1) * LANES] = piece.astype(out_ref.dtype)
 
@@ -512,7 +568,7 @@
 
 def group_sizes(bundles):
     if bundles == 8:
-        return [2, 3, 2, 1]
+        return [2, 2, 3, 1]
     return [1] * bundles
 
 
@@ -548,6 +604,7 @@
     def do_back(group):
         if group < groups:
             near[group] = gate(near[group], done["last"])
+            done["last"] = [near[group]]
             back[group] = moved(near[group], back_pairs)
 
     def do_pick(group):
@@ -570,7 +627,7 @@
         running = jnp.cumsum(log_decay, axis=0)
         light["cols"] = running.reshape(rows, bundles, BUNDLE).transpose(1, 0, 2)
         light["rows"] = running.T.reshape(bundles, BUNDLE, rows)
-        exact, first, sent = local_state(key1, value1, light["cols"], done["last"])
+        exact, first, sent = local_state(key1, value1, light["rows"], done["last"])
         light["first"] = first
         light["other"] = moved(sent, swap_pairs)
         light["exact"] = exact
@@ -620,30 +677,29 @@
         done["last"] = done["last"] + [chip[group]]
 
     do_pack(0)
+    do_pack(1)
     do_state()
-    do_pack(1)
     do_back(0)
     do_mix_local()
     wait_chip(0)
     do_chip()
+    do_back(1)
     do_pick(0)
     do_join()
     do_attend(0)
     do_join()
-    do_back(1)
-    wait_chip(1)
     do_join()
     do_pack(2)
+    do_pick(1)
     do_mix_final()
-    do_pick(1)
     do_project()
     do_back(2)
     do_pack(3)
     do_attend(1)
     do_back(3)
     do_pick(2)
+    do_attend(2)
     do_pick(3)
-    do_attend(2)
     do_attend(3)
     return (done["linear"], done["attended"])
 

time: 352 us -> 662 us (1.88)
  Pallas kernels: 140 us -> 541 us
  waiting for transfers between devices: 109 us -> 40.1 us
  local copies, waits for them, and re-layouts: 19.9 us -> 8.63 us
  starting transfers between devices: 45.7 us -> 34.8 us
    pallas_call x11, Pallas kernels: 35.2 us -> 399 us  [the longest x4 195 us: pack(): pl.pallas_call(functools.partial(pack_kernel, base), in_specs=untouched([...]
    ppermute x21, waiting for transfers between devices: 109 us -> 40.1 us  [moved(): lax.ppermute(value, 'ctx', [(s, t) for s, t in pairs if 0 <= t < count])]
    pallas_call x4, Pallas kernels: 58.2 us -> 98.7 us  [attend(): pl.pallas_call(attend_kernel, grid_spec=pltpu.PrefetchScalarGridSpec(num_...]
    unnamed x37 -> x22, local copies, waits for them, and re-layouts: 17 us -> 5.73 us
    ppermute x21, starting transfers between devices: 45.7 us -> 34.8 us  [moved(): lax.ppermute(value, 'ctx', [(s, t) for s, t in pairs if 0 <= t < count])]
  transfers between devices with their start and end apart: 22 -> 22, of which waited for: 6 -> 6; matrix products, arithmetic and copies ran while one was open for 7% -> 3% of each run, Pallas kernels for 40% -> 68%
where the time goes in v1:
time: 662 us; the launch traced here: 656 us
  Pallas kernels  541 us (82%)
  waiting for transfers between devices  40.1 us (6%)
  starting transfers between devices  34.8 us (5%)
  matrix products  15.9 us (2%)
  between operations  14.6 us (2%)
  local copies, waits for them, and re-layouts  8.63 us (1%)
    pallas_call x4, Pallas kernels, pack(): pl.pallas_call(functools.partial(pack_kernel, base), in_specs=untouched([...  195 us
    pallas_call x4, Pallas kernels, pick(): pl.pallas_call(pick_kernel, in_specs=[pl.BlockSpec(memory_space=pltpu.SME...  195 us
    pallas_call x4, Pallas kernels, attend(): pl.pallas_call(attend_kernel, grid_spec=pltpu.PrefetchScalarGridSpec(num_...  98.7 us
    ppermute x21, waiting for transfers between devices, moved(): lax.ppermute(value, 'ctx', [(s, t) for s, t in pairs if 0 <= t < count])  40.1 us
    ppermute x21, starting transfers between devices, moved(): lax.ppermute(value, 'ctx', [(s, t) for s, t in pairs if 0 <= t < count])  34.8 us
    pallas_call x1, Pallas kernels, mix_final(): pl.pallas_call(functools.partial(mix_final_kernel, half), grid_spec=pltpu...  17 us
    dot_general x1, matrix products, do_project(): jnp.dot(light['normed'], out_weight, preferred_element_type=jnp.float32)  15.9 us
    pallas_call x1, Pallas kernels, mix_local(): pl.pallas_call(mix_local_kernel, grid=(width // WIDE,), in_specs=[block,...  14 us
  transfers between devices with their start and end apart: 22, of which 6 were waited for; matrix products, arithmetic and copies ran while one was open for 3% of the time, Pallas kernels for 68%

profile of v1, /device:TPU:25, one launch (start us, length us, event | category | flops | bytes accessed | tf_op | source)
XLA Modules:
  0.0 656.4 jit_solution(3691927058283872216)
XLA Ops:
  7.2 0.0 copy-start
  7.2 0.0 reduce-scatter.2.cloned.1.call-start
  7.2 48.8 %pack.4.rest_0_ = bf16[2,512,768]{2,1,0:T(8,128)(2,1)} custom-call(bf16[512,3072]{1,0:T(8,128)(2,1)} %key_ref.19, bf16[512,3072]{1,0:T(8,128)(2,1)} %value_ref.19), custom_call_target="tpu_custom_call" | custom-call | flops 1000 | bytes 1000 | tf_op jit(solution)/shard_map/pack/pallas_call | solution.py:70
  56.0 1.3 collective-permute-start
  57.3 4.4 collective-permute-start.2
  61.7 48.8 %pack.5.rest_0_ = bf16[2,512,768]{2,1,0:T(8,128)(2,1)} custom-call(bf16[512,3072]{1,0:T(8,128)(2,1)} %key_ref.19, bf16[512,3072]{1,0:T(8,128)(2,1)} %value_ref.19, bf16[2,512,768]{2,1,0:T(8,128)(2,1)} %pack.4.rest_0_), custom_call_target="tpu_custom_call" | custom-call | flops 1000 | bytes 1000 | tf_op jit(solution)/shard_map/pack/pallas_call | solution.py:70
  110.5 1.3 collective-permute-start.5
  111.8 1.2 reduce-window.6
  113.0 0.2 slice_reduce_fusion
  113.2 0.1 broadcast_add_fusion
  113.3 0.7 reduce_window_sum.21.decay_ref.row_ref
  114.0 9.3 %local_state.1 = (f32[32,96,128]{2,1,0:T(8,128)}, f32[32,96,128]{2,1,0:T(8,128)}, bf16[32,96,128]{2,1,0:T(8,128)(2,1)}) custom-call(bf16[512,3072]{1,0:T(8,128)(2,1)} %key_ref.13, bf16[512,3072]{1,0:T(8,128)(2,1)} %value_ref.13, f32[8,4,512]{2,1,0:T(4,128)} %reduce_window_sum.21.decay_ref.row_ref, bf16[2,512,768]{2,1,0:T(8,128)(2,1)} %pack.5.rest_0_), custom_call_target="tpu_custom_call" | custom-call | flops 1000 | bytes 1000 | tf_op jit(solution)/shard_map/local_state/pallas_call | solution.py:372
  123.3 1.3 collective-permute-start.4
  124.6 1.7 collective-permute-start.1
  126.3 0.1 bitcast_bitcast_fusion
  126.4 2.0 copy.21
  128.4 14.0 %mix_local.1.rest_0_.local_ref = f32[512,3072]{1,0:T(8,128)} custom-call(bf16[512,3072]{1,0:T(8,128)(2,1)} %query_ref.8, bf16[512,3072]{1,0:T(8,128)(2,1)} %key_ref.13, bf16[512,3072]{1,0:T(8,128)(2,1)} %value_ref.13, f32[8,512,4]{2,1,0:T(8,128)} %bitcast.19, f32[8,4,512]{2,1,0:T(4,128)} %reduce_window_sum.21.decay_ref.row_ref, ...), custom_call_target="tpu_custom_call" | custom-call | flops 1000 | bytes 1000 | tf_op jit(solution)/shard_map/mix_local/pallas_call | solution.py:492
  142.4 0.9 copy-done.4
  143.2 2.7 chip_state.1
  145.9 48.8 %pick.4.rest_0_.mid_ref = bf16[2,512,768]{2,1,0:T(8,128)(2,1)} custom-call(s32[1]{0:T(128)} %bitcast.info, bf16[2,512,768]{2,1,0:T(8,128)(2,1)} %collective-permute-done.2.rest_1_.chip_ref, bf16[2,512,768]{2,1,0:T(8,128)(2,1)} %collective-permute-done.4.back_ref, bf16[2,512,768]{2,1,0:T(8,128)(2,1)} %gate.5.rest_0_.near_ref), custom_call_target="tpu_custom_call" | custom-call | flops 1000 | bytes 1000 | tf_op jit(solution)/shard_map/pick/pallas_call | solution.py:100
  194.7 0.1 collective-permute-start.7
  194.8 3.9 collective-permute-start.3
  198.7 2.6 collective-permute-start.10
  201.2 1.3 collective-permute-start.11
  202.5 8.2 %collective-permute-done.3.arrived_ref = bf16[16,96,128]{2,1,0:T(8,128)(2,1)S(1)} collective-permute-done((bf16[16,96,128]{2,1,0:T(8,128)(2,1)S(1)}, bf16[16,96,128]{2,1,0:T(8,128)(2,1)S(1)}, u32[]{:S(2)}, u32[]{:S(2)}) %collective-permute-start.3) | collective-permute-done | bytes 393248 | tf_op jit(solution)/shard_map/ppermute | solution.py:583
  210.8 0.7 copy-done.7
  211.5 3.2 join.3
  214.7 1.3 collective-permute-start.6
  216.0 31.3 %attend.4.rest_0_ = bf16[512,3072]{1,0:T(8,128)(2,1)} custom-call(s32[1]{0:T(128)} %bitcast.info, bf16[512,3072]{1,0:T(8,128)(2,1)} %query_ref.11, bf16[512,3072]{1,0:T(8,128)(2,1)} %key_ref.19, bf16[512,3072]{1,0:T(8,128)(2,1)} %value_ref.19, bf16[2,512,768]{2,1,0:T(8,128)(2,1)} %gate.4.rest_0_.near_ref, bf16[2,512,768]{2,1,0:T(8,128)(2,1)} %pick.4.rest_0_.mid_ref, ...), custom_call_target="tpu_custom_call" | custom-call | flops 1000 | bytes 1000 | tf_op jit(solution)/shard_map/attend/pallas_call | solution.py:280
  247.3 0.8 copy-done.8
  248.1 3.1 join.4
  251.3 1.3 collective-permute-start.8
  252.5 19.7 %collective-permute-done.8.arrived_ref = bf16[16,96,128]{2,1,0:T(8,128)(2,1)S(1)} collective-permute-done((bf16[16,96,128]{2,1,0:T(8,128)(2,1)}, bf16[16,96,128]{2,1,0:T(8,128)(2,1)S(1)}, u32[]{:S(2)}, u32[]{:S(2)}) %collective-permute-start.8) | collective-permute-done | bytes 393248 | tf_op jit(solution)/shard_map/ppermute | solution.py:583
  272.2 0.8 copy-done.9
  273.0 3.0 join.5
  276.0 2.0 collective-permute-start.9
  278.0 72.6 %pack.6.rest_0_ = bf16[2,512,1152]{2,1,0:T(8,128)(2,1)} custom-call(bf16[512,3072]{1,0:T(8,128)(2,1)} %key_ref.19, bf16[512,3072]{1,0:T(8,128)(2,1)} %value_ref.19, bf16[16,96,128]{2,1,0:T(8,128)(2,1)} %get-tuple-element.27.rest_0_), custom_call_target="tpu_custom_call" | custom-call | flops 1000 | bytes 1000 | tf_op jit(solution)/shard_map/pack/pallas_call | solution.py:70
  350.6 1.3 collective-permute-start.12
  351.9 48.8 %pick.5.rest_0_.mid_ref = bf16[2,512,768]{2,1,0:T(8,128)(2,1)} custom-call(s32[1]{0:T(128)} %bitcast.info, bf16[2,512,768]{2,1,0:T(8,128)(2,1)} %collective-permute-done.10.chip_ref, bf16[2,512,768]{2,1,0:T(8,128)(2,1)} %collective-permute-done.11.back_ref, bf16[2,512,1152]{2,1,0:T(8,128)(2,1)} %pack.6.rest_0_), custom_call_target="tpu_custom_call" | custom-call | flops 1000 | bytes 1000 | tf_op jit(solution)/shard_map/pick/pallas_call | solution.py:100
  400.7 0.0 copy-start.10
  400.7 0.7 copy-done.10
  401.4 17.0 %mix_final.1 = bf16[512,3072]{1,0:T(8,128)(2,1)} custom-call(s32[1]{0:T(128)} %bitcast.info, bf16[512,3072]{1,0:T(8,128)(2,1)} %query_ref.8, f32[512,3072]{1,0:T(8,128)} %mix_local.1.rest_0_.local_ref, f32[8,512,4]{2,1,0:T(8,128)} %bitcast.20, f32[16,96,128]{2,1,0:T(8,128)} %get-tuple-element.26.own_ref, bf16[16,96,128]{2,1,0:T(8,128)(2,1)} %copy-done.10, ...), custom_call_target="tpu_custom_call" | custom-call | flops 1000 | bytes 1000 | tf_op jit(solution)/shard_map/mix_final/pallas_call | solution.py:546
  418.4 15.9 %convolution_convert_fusion.refs_1_ = bf16[512,3072]{1,0:T(8,128)(2,1)} fusion(bf16[512,3072]{1,0:T(8,128)(2,1)} %mix_final.1, bf16[3072,3072]{1,0:T(8,128)(2,1)} %param.12), kind=kOutput, calls=%fused_computation | convolution fusion | flops 9665249280 | bytes 25165824 | tf_op jit(solution)/shard_map/dot_general | solution.py:671
  434.3 0.0 reduce-scatter.2.cloned.1.call-update
  434.3 3.5 collective-permute-start.17
  437.8 1.3 collective-permute-start.18
  439.1 0.8 collective-permute-start.14
  439.9 24.9 %pack.7.rest_1_ = bf16[2,512,384]{2,1,0:T(8,128)(2,1)} custom-call(bf16[512,3072]{1,0:T(8,128)(2,1)} %key_ref.19, bf16[512,3072]{1,0:T(8,128)(2,1)} %value_ref.19, bf16[2,512,1152]{2,1,0:T(8,128)(2,1)} %gate.6.rest_0_.near_ref), custom_call_target="tpu_custom_call" | custom-call | flops 1000 | bytes 1000 | tf_op jit(solution)/shard_map/pack/pallas_call | solution.py:70
  464.9 1.3 collective-permute-start.13
  466.2 15.9 %attend.5.refs_1_.rest_0_ = bf16[512,3072]{1,0:T(8,128)(2,1)} custom-call(s32[1]{0:T(128)} %bitcast.info, bf16[512,3072]{1,0:T(8,128)(2,1)} %query_ref.11, bf16[512,3072]{1,0:T(8,128)(2,1)} %key_ref.19, bf16[512,3072]{1,0:T(8,128)(2,1)} %value_ref.19, bf16[2,512,768]{2,1,0:T(8,128)(2,1)} %gate.5.rest_0_.near_ref, ...), custom_call_target="tpu_custom_call", output_to_operand_aliasing={{}: (7, {})} | custom-call | flops 1000 | bytes 1000 | tf_op jit(solution)/shard_map/attend/pallas_call | solution.py:280
  482.1 0.9 copy-done.2
  483.0 3.1 collective-permute-done.17.chip_ref
  486.1 5.8 collective-permute-done.18.back_ref
  491.9 72.6 %pick.6.mid_ref.rest_1_ = bf16[2,512,1152]{2,1,0:T(8,128)(2,1)} custom-call(s32[1]{0:T(128)} %bitcast.info, bf16[2,512,1152]{2,1,0:T(8,128)(2,1)} %collective-permute-done.17.chip_ref, bf16[2,512,1152]{2,1,0:T(8,128)(2,1)} %collective-permute-done.18.back_ref, bf16[2,512,384]{2,1,0:T(8,128)(2,1)} %gate.7.rest_0_.near_ref), custom_call_target="tpu_custom_call" | custom-call | flops 1000 | bytes 1000 | tf_op jit(solution)/shard_map/pick/pallas_call | solution.py:100
  564.5 0.1 collective-permute-start.19
  564.6 2.7 collective-permute-start.15
  567.3 1.3 collective-permute-start.16
  568.6 0.8 collective-permute-done.19.swap_ref
  569.5 37.5 %attend.6.rest_0_ = bf16[512,3072]{1,0:T(8,128)(2,1)} custom-call(s32[1]{0:T(128)} %bitcast.info, bf16[512,3072]{1,0:T(8,128)(2,1)} %query_ref.11, bf16[512,3072]{1,0:T(8,128)(2,1)} %key_ref.19, bf16[512,3072]{1,0:T(8,128)(2,1)} %value_ref.19, bf16[2,512,1152]{2,1,0:T(8,128)(2,1)} %gate.6.rest_0_.near_ref, ...), custom_call_target="tpu_custom_call", output_to_operand_aliasing={{}: (7, {})} | custom-call | flops 1000 | bytes 1000 | tf_op jit(solution)/shard_map/attend/pallas_call | solution.py:280
  607.0 24.9 %pick.7.mid_ref.rest_1_ = bf16[2,512,384]{2,1,0:T(8,128)(2,1)} custom-call(s32[1]{0:T(128)} %bitcast.info, bf16[2,512,384]{2,1,0:T(8,128)(2,1)} %collective-permute-done.15.chip_ref, bf16[2,512,384]{2,1,0:T(8,128)(2,1)} %collective-permute-done.16.back_ref, bf16[512,3072]{1,0:T(8,128)(2,1)} %attend.6.rest_0_), custom_call_target="tpu_custom_call" | custom-call | flops 1000 | bytes 1000 | tf_op jit(solution)/shard_map/pick/pallas_call | solution.py:100
  632.0 0.2 collective-permute-start.20
  632.2 2.4 collective-permute-done.20.swap_ref
  634.5 0.9 copy-done.5
  635.4 13.9 %attend.7 = bf16[512,3072]{1,0:T(8,128)(2,1)} custom-call(s32[1]{0:T(128)} %bitcast.info, bf16[512,3072]{1,0:T(8,128)(2,1)} %query_ref.11, bf16[512,3072]{1,0:T(8,128)(2,1)} %key_ref.19, bf16[512,3072]{1,0:T(8,128)(2,1)} %value_ref.19, bf16[2,512,384]{2,1,0:T(8,128)(2,1)} %gate.7.rest_0_.near_ref, ...), custom_call_target="tpu_custom_call", output_to_operand_aliasing={{}: (7, {})} | custom-call | flops 1000 | bytes 1000 | tf_op jit(solution)/shard_map/attend/pallas_call | solution.py:280
  (38 shorter events, 0.2 us)
Async XLA Ops:
  7.2 104.6 %copy-start = (f32[512,32]{0,1:T(8,128)S(1)}, f32[512,32]{0,1:T(8,128)}, u32[]{:S(2)}) copy-start(f32[512,32]{0,1:T(8,128)} %param.11) | copy-start | bytes 196612
  7.2 642.2 %reduce-scatter.2.cloned.1.call-start = ((), (), s32[]{:S(2)}) async-start(), calls=%async_computation.1 | async-start | bytes 4718592 | tf_op jit(solution)/shard_map/reduce_scatter | solution.py:673
  56.0 67.3 %collective-permute-start = (bf16[2,512,768]{2,1,0:T(8,128)(2,1)}, bf16[2,512,768]{2,1,0:T(8,128)(2,1)}, u32[]{:S(2)}, u32[]{:S(2)}) collective-permute-start(bf16[2,512,768]{2,1,0:T(8,128)(2,1)} %pack.4.rest_0_), channel_id=1, source_target_pairs={{0,2},{2,8},{4,6},{6,12},{8,10},{10,16},{12,14},{14,20},{16,18},{1... | collective-permute-start | bytes 4718600 | tf_op jit(solution)/shard_map/ppermute | solution.py:583
  57.3 85.0 %collective-permute-start.2 = (bf16[2,512,768]{2,1,0:T(8,128)(2,1)}, bf16[2,512,768]{2,1,0:T(8,128)(2,1)}, u32[]{:S(2)}, u32[]{:S(2)}) collective-permute-start(bf16[2,512,768]{2,1,0:T(8,128)(2,1)} %pack.4.rest_0_), channel_id=1, source_target_pairs={{0,4},{2,6},{4,8},{8,12},{10,14},{12,16},{16,20},{18,22},{20,24},{... | collective-permute-start | bytes 4718600 | tf_op jit(solution)/shard_map/ppermute | solution.py:583
  110.5 35.4 %collective-permute-start.5 = (bf16[2,512,768]{2,1,0:T(8,128)(2,1)}, bf16[2,512,768]{2,1,0:T(8,128)(2,1)}, u32[]{:S(2)}, u32[]{:S(2)}) collective-permute-start(bf16[2,512,768]{2,1,0:T(8,128)(2,1)} %pack.5.rest_0_), channel_id=1, source_target_pairs={{0,2},{2,8},{4,6},{6,12},{8,10},{10,16},{12,14},{14,20},{16,18},{1... | collective-permute-start | bytes 4718600 | tf_op jit(solution)/shard_map/ppermute | solution.py:583
  123.3 22.6 %collective-permute-start.4 = (bf16[2,512,768]{2,1,0:T(8,128)(2,1)}, bf16[2,512,768]{2,1,0:T(8,128)(2,1)}, u32[]{:S(2)}, u32[]{:S(2)}) collective-permute-start(bf16[2,512,768]{2,1,0:T(8,128)(2,1)} %gate.4.rest_0_.near_ref), channel_id=1, source_target_pairs={{12,10},{20,18},{28,26},{13,11},{21,19},{29,27}} | collective-permute-start | bytes 4718600 | tf_op jit(solution)/shard_map/ppermute | solution.py:583
  124.6 17.8 %collective-permute-start.1 = (bf16[32,96,128]{2,1,0:T(8,128)(2,1)}, bf16[32,96,128]{2,1,0:T(8,128)(2,1)S(1)}, u32[]{:S(2)}, u32[]{:S(2)}) collective-permute-start(bf16[32,96,128]{2,1,0:T(8,128)(2,1)} %get-tuple-element.16.refs_1_), channel_id=1, source_target_pairs={{0,2},{2,0},{4,6},{6,4},{8,10},{10,8},{12,14},{14,12},{16,18},{18,... | collective-permute-start | bytes 2359304 | tf_op jit(solution)/shard_map/ppermute | solution.py:583
  142.3 0.9 copy-start.4
  145.9 48.9 %copy-start.6 = (bf16[16,96,128]{2,1,0:T(8,128)(2,1)S(1)}, bf16[16,96,128]{2,1,0:T(8,128)(2,1)}, u32[]{:S(2)}) copy-start(bf16[16,96,128]{2,1,0:T(8,128)(2,1)} %get-tuple-element.19.refs_1_) | copy-start | bytes 1179652
  194.7 21.3 %collective-permute-start.7 = (bf16[2,512,768]{2,1,0:T(8,128)(2,1)}, bf16[2,512,768]{2,1,0:T(8,128)(2,1)}, u32[]{:S(2)}, u32[]{:S(2)}) collective-permute-start(bf16[2,512,768]{2,1,0:T(8,128)(2,1)} %pick.4.rest_0_.mid_ref), channel_id=1, source_target_pairs={{0,2},{2,0},{4,6},{6,4},{8,10},{10,8},{12,14},{14,12},{16,18},{18,... | collective-permute-start | bytes 4718600 | tf_op jit(solution)/shard_map/ppermute | solution.py:583
  194.8 16.0 %collective-permute-start.3 = (bf16[16,96,128]{2,1,0:T(8,128)(2,1)S(1)}, bf16[16,96,128]{2,1,0:T(8,128)(2,1)S(1)}, u32[]{:S(2)}, u32[]{:S(2)}) collective-permute-start(bf16[16,96,128]{2,1,0:T(8,128)(2,1)S(1)} %copy-done.6), channel_id=1, source_target_pairs={{0,4},{2,6},{4,8},{6,10},{8,12},{10,14},{12,16},{14,18},{16,20},{1... | collective-permute-start | bytes 1179656 | tf_op jit(solution)/shard_map/ppermute | solution.py:583
  198.7 153.2 %collective-permute-start.10 = (bf16[2,512,768]{2,1,0:T(8,128)(2,1)}, bf16[2,512,768]{2,1,0:T(8,128)(2,1)}, u32[]{:S(2)}, u32[]{:S(2)}) collective-permute-start(bf16[2,512,768]{2,1,0:T(8,128)(2,1)} %pack.5.rest_0_), channel_id=1, source_target_pairs={{0,4},{2,6},{4,8},{8,12},{10,14},{12,16},{16,20},{18,22},{20,24},{... | collective-permute-start | bytes 4718600 | tf_op jit(solution)/shard_map/ppermute | solution.py:583
  201.2 150.7 %collective-permute-start.11 = (bf16[2,512,768]{2,1,0:T(8,128)(2,1)}, bf16[2,512,768]{2,1,0:T(8,128)(2,1)}, u32[]{:S(2)}, u32[]{:S(2)}) collective-permute-start(bf16[2,512,768]{2,1,0:T(8,128)(2,1)} %gate.5.rest_0_.near_ref), channel_id=1, source_target_pairs={{12,10},{20,18},{28,26},{13,11},{21,19},{29,27}} | collective-permute-start | bytes 4718600 | tf_op jit(solution)/shard_map/ppermute | solution.py:583
  210.8 0.7 copy-start.7
  214.7 32.6 %collective-permute-start.6 = (bf16[16,96,128]{2,1,0:T(8,128)(2,1)}, bf16[16,96,128]{2,1,0:T(8,128)(2,1)S(1)}, u32[]{:S(2)}, u32[]{:S(2)}) collective-permute-start(bf16[16,96,128]{2,1,0:T(8,128)(2,1)} %get-tuple-element.22.rest_0_), channel_id=1, source_target_pairs={{0,8},{2,10},{4,12},{6,14},{8,16},{10,18},{12,20},{14,22},{16,24},... | collective-permute-start | bytes 1179656 | tf_op jit(solution)/shard_map/ppermute | solution.py:583
  247.3 0.8 copy-start.8
  251.3 21.0 %collective-permute-start.8 = (bf16[16,96,128]{2,1,0:T(8,128)(2,1)}, bf16[16,96,128]{2,1,0:T(8,128)(2,1)S(1)}, u32[]{:S(2)}, u32[]{:S(2)}) collective-permute-start(bf16[16,96,128]{2,1,0:T(8,128)(2,1)} %get-tuple-element.25.rest_0_), channel_id=1, source_target_pairs={{0,16},{2,18},{4,20},{6,22},{8,24},{10,26},{12,28},{14,30},{1,17},... | collective-permute-start | bytes 1179656 | tf_op jit(solution)/shard_map/ppermute | solution.py:583
  272.2 0.8 copy-start.9
  276.0 124.7 %collective-permute-start.9 = (bf16[16,96,128]{2,1,0:T(8,128)(2,1)}, bf16[16,96,128]{2,1,0:T(8,128)(2,1)S(1)}, u32[]{:S(2)}, u32[]{:S(2)}) collective-permute-start(bf16[16,96,128]{2,1,0:T(8,128)(2,1)} %get-tuple-element.27.rest_0_), channel_id=1, source_target_pairs={{0,2},{2,0},{4,6},{6,4},{8,10},{10,8},{12,14},{14,12},{16,18},{18,... | collective-permute-start | bytes 1179656 | tf_op jit(solution)/shard_map/ppermute | solution.py:583
  350.6 87.2 %collective-permute-start.12 = (bf16[2,512,1152]{2,1,0:T(8,128)(2,1)}, bf16[2,512,1152]{2,1,0:T(8,128)(2,1)}, u32[]{:S(2)}, u32[]{:S(2)}) collective-permute-start(bf16[2,512,1152]{2,1,0:T(8,128)(2,1)} %pack.6.rest_0_), channel_id=1, source_target_pairs={{0,2},{2,8},{4,6},{6,12},{8,10},{10,16},{12,14},{14,20},{16,18},{1... | collective-permute-start | bytes 7077896 | tf_op jit(solution)/shard_map/ppermute | solution.py:583
  400.7 0.7 copy-start.10
  434.3 51.8 %collective-permute-start.17 = (bf16[2,512,1152]{2,1,0:T(8,128)(2,1)}, bf16[2,512,1152]{2,1,0:T(8,128)(2,1)}, u32[]{:S(2)}, u32[]{:S(2)}) collective-permute-start(bf16[2,512,1152]{2,1,0:T(8,128)(2,1)} %pack.6.rest_0_), channel_id=1, source_target_pairs={{0,4},{2,6},{4,8},{8,12},{10,14},{12,16},{16,20},{18,22},{20,24},{... | collective-permute-start | bytes 7077896 | tf_op jit(solution)/shard_map/ppermute | solution.py:583
  437.8 54.1 %collective-permute-start.18 = (bf16[2,512,1152]{2,1,0:T(8,128)(2,1)}, bf16[2,512,1152]{2,1,0:T(8,128)(2,1)}, u32[]{:S(2)}, u32[]{:S(2)}) collective-permute-start(bf16[2,512,1152]{2,1,0:T(8,128)(2,1)} %gate.6.rest_0_.near_ref), channel_id=1, source_target_pairs={{12,10},{20,18},{28,26},{13,11},{21,19},{29,27}} | collective-permute-start | bytes 7077896 | tf_op jit(solution)/shard_map/ppermute | solution.py:583
  439.1 27.1 %collective-permute-start.14 = (bf16[2,512,768]{2,1,0:T(8,128)(2,1)}, bf16[2,512,768]{2,1,0:T(8,128)(2,1)}, u32[]{:S(2)}, u32[]{:S(2)}) collective-permute-start(bf16[2,512,768]{2,1,0:T(8,128)(2,1)} %pick.5.rest_0_.mid_ref), channel_id=1, source_target_pairs={{0,2},{2,0},{4,6},{6,4},{8,10},{10,8},{12,14},{14,12},{16,18},{18,... | collective-permute-start | bytes 4718600 | tf_op jit(solution)/shard_map/ppermute | solution.py:583
  464.9 17.3 %collective-permute-start.13 = (bf16[2,512,384]{2,1,0:T(8,128)(2,1)}, bf16[2,512,384]{2,1,0:T(8,128)(2,1)S(1)}, u32[]{:S(2)}, u32[]{:S(2)}) collective-permute-start(bf16[2,512,384]{2,1,0:T(8,128)(2,1)} %pack.7.rest_1_), channel_id=1, source_target_pairs={{0,2},{2,8},{4,6},{6,12},{8,10},{10,16},{12,14},{14,20},{16,18},{1... | collective-permute-start | bytes 2359304 | tf_op jit(solution)/shard_map/ppermute | solution.py:583
  482.1 0.9 copy-start.2
  483.0 84.3 %copy-start.3 = (bf16[2,512,384]{2,1,0:T(8,128)(2,1)S(1)}, bf16[2,512,384]{2,1,0:T(8,128)(2,1)}, u32[]{:S(2)}) copy-start(bf16[2,512,384]{2,1,0:T(8,128)(2,1)} %gate.7.rest_0_.near_ref) | copy-start | bytes 2359300
  564.5 4.9 collective-permute-start.19
  564.6 42.4 %collective-permute-start.15 = (bf16[2,512,384]{2,1,0:T(8,128)(2,1)}, bf16[2,512,384]{2,1,0:T(8,128)(2,1)}, u32[]{:S(2)}, u32[]{:S(2)}) collective-permute-start(bf16[2,512,384]{2,1,0:T(8,128)(2,1)} %pack.7.rest_1_), channel_id=1, source_target_pairs={{0,4},{2,6},{4,8},{8,12},{10,14},{12,16},{16,20},{18,22},{20,24},{... | collective-permute-start | bytes 2359304 | tf_op jit(solution)/shard_map/ppermute | solution.py:583
  567.3 39.7 %collective-permute-start.16 = (bf16[2,512,384]{2,1,0:T(8,128)(2,1)S(1)}, bf16[2,512,384]{2,1,0:T(8,128)(2,1)}, u32[]{:S(2)}, u32[]{:S(2)}) collective-permute-start(bf16[2,512,384]{2,1,0:T(8,128)(2,1)S(1)} %copy-done.3), channel_id=1, source_target_pairs={{12,10},{20,18},{28,26},{13,11},{21,19},{29,27}} | collective-permute-start | bytes 2359304 | tf_op jit(solution)/shard_map/ppermute | solution.py:583
  632.0 2.6 collective-permute-start.20
  634.5 0.9 copy-start.5
  635.4 13.9 %copy-start.1 = (f32[512,32]{0,1:T(8,128)S(1)}, f32[512,32]{0,1:T(8,128)}, u32[]{:S(2)}) copy-start(f32[512,32]{0,1:T(8,128)} %param.11) | copy-start | bytes 196612
Sparse Core Ops, SparseCore 0:
  434.4 43.8 reduce-scatter.1

commit v2 on v0

--- a/solution.py
+++ b/solution.py
@@ -14,7 +14,7 @@
 WIDE = BUNDLE * DH
 LANES = 128
 EPS_NORM = 1e-06
-VMEM_BYTES = 60 * 1024 * 1024
+VMEM_BYTES = 63 * 1024 * 1024
 WINDOWS = ((0, 128, 0), (0, 256, 96), (128, 256, 64), (256, 128, 32))
 
 
@@ -27,7 +27,7 @@
 
 
 def untouched(deps):
-    return [pl.BlockSpec(memory_space=pltpu.HBM)] * len(deps)
+    return [pl.BlockSpec(memory_space=pl.ANY)] * len(deps)
 
 
 def gate_kernel(*refs):
@@ -38,7 +38,7 @@
     return pl.pallas_call(
         gate_kernel,
         in_specs=untouched([value, *deps]),
-        out_specs=pl.BlockSpec(memory_space=pltpu.HBM),
+        out_specs=pl.BlockSpec(memory_space=pl.ANY),
         out_shape=jax.ShapeDtypeStruct(value.shape, value.dtype),
         input_output_aliases={0: 0},
         compiler_params=params(),
@@ -88,22 +88,24 @@
 
 def pick(info, chip, back, deps):
     _, rows, width = chip.shape
-    shape = (2, rows, WIDE)
-
-    def from_chip(b, info):
-        return (0, 0, jnp.where(lax.rem(info[0], 4) == 1, 0, b))
-
-    def from_back(b, info):
-        return (0, 0, jnp.where(lax.rem(info[0], 4) == 1, b, 0))
+    shape = (1, rows, WIDE)
+
+    def from_chip(i, b, info):
+        other = lax.rem(info[0], 4) == 1
+        return (jnp.where(other, 0, i), 0, jnp.where(other, 0, b))
+
+    def from_back(i, b, info):
+        other = lax.rem(info[0], 4) != 1
+        return (jnp.where(other, 0, i), 0, jnp.where(other, 0, b))
 
     return pl.pallas_call(
         pick_kernel,
         grid_spec=pltpu.PrefetchScalarGridSpec(
             num_scalar_prefetch=1,
-            grid=(width // WIDE,),
+            grid=(2, width // WIDE),
             in_specs=[pl.BlockSpec(shape, from_chip), pl.BlockSpec(shape, from_back)]
             + untouched(deps),
-            out_specs=pl.BlockSpec(shape, lambda b, _: (0, 0, b)),
+            out_specs=pl.BlockSpec(shape, lambda i, b, _: (i, 0, b)),
         ),
         out_shape=jax.ShapeDtypeStruct(chip.shape, chip.dtype),
         compiler_params=params(),
@@ -115,18 +117,20 @@
 def attend_body(exists, query_ref, slots, out_ref):
     rows = query_ref.shape[0]
     scale = math.log2(math.e) / math.sqrt(DH)
-    row = lax.broadcasted_iota(jnp.int32, (SUB, SUB), 0)
-    col = lax.broadcasted_iota(jnp.int32, (SUB, SUB), 1)
-    newer, older = col > row, col <= row
+    key_at = lax.broadcasted_iota(jnp.int32, (SUB, SUB), 0)
+    query_at = lax.broadcasted_iota(jnp.int32, (SUB, SUB), 1)
+    newer, older = key_at > query_at, key_at <= query_at
     low = jnp.float32(-1e30)
-    units = [(part, window) for part in range(rows // SUB) for window in WINDOWS]
+    values = [value_ref[...].T for _, value_ref in slots]
+    ones = jnp.ones((16, rows), values[0].dtype)
+    units = [(part, head) for part in range(rows // SUB) for head in range(BUNDLE)]
 
     def spans(part):
         first = part * SUB
         return [(first, rows), (0, rows), (0, rows), (0, first + SUB)]
 
-    def score_unit(part, window):
-        start, width, place = window
+    def score_unit(part, head):
+        start, width, place = WINDOWS[head]
         lanes = slice(start, start + width)
         query = query_ref[part * SUB : (part + 1) * SUB, lanes]
         query = jnp.where(head_lanes(query.shape, place), query, jnp.zeros_like(query))
@@ -137,8 +141,8 @@
             top = None
             for at in range(begin, end, SUB):
                 score = lax.dot_general(
+                    slots[slot][0][at : at + SUB, lanes],
                     query,
-                    slots[slot][0][at : at + SUB, lanes],
                     (((1,), (1,)), ((), ())),
                     preferred_element_type=jnp.float32,
                 )
@@ -147,48 +151,37 @@
                 if slot == 3 and at == end - SUB:
                     score = jnp.where(older, score, low)
                 tiles[slot].append(score)
-                for lane in range(0, SUB, LANES):
-                    piece = score[:, lane : lane + LANES]
-                    top = piece if top is None else jnp.maximum(top, piece)
+                piece = jnp.max(score, axis=0, keepdims=True)
+                top = piece if top is None else jnp.maximum(top, piece)
             if slot < 3:
                 top = jnp.where(exists[slot], top, low)
             peak = top if peak is None else jnp.maximum(peak, top)
-        return tiles, jnp.max(peak, axis=1, keepdims=True) * scale
-
-    def value_unit(part, window, tiles, peak):
-        start, width, place = window
-        lanes = slice(start, start + width)
+        return tiles, peak * scale
+
+    def value_unit(part, head, tiles, peak):
         result = None
         for slot in range(4):
             begin, end = spans(part)[slot]
             shift = peak
             if slot < 3:
                 shift = jnp.where(exists[slot], peak, jnp.float32(1e30))
-            for index, at in enumerate(range(begin, end, SUB)):
-                weight = jnp.exp2(tiles[slot][index] * scale - shift).astype(jnp.bfloat16)
-                value = slots[slot][1][at : at + SUB, lanes]
-                value = jnp.where(head_lanes(value.shape, place), value, jnp.ones_like(value))
-                term = jnp.dot(weight, value, preferred_element_type=jnp.float32)
-                result = term if result is None else result + term
-        spare = 96 if place == 0 else 0
-        result = result * (1.0 / result[:, spare : spare + 1])
-        return jnp.where(head_lanes(result.shape, place), result, 0.0)
+            weights = [jnp.exp2(tile * scale - shift).astype(jnp.bfloat16) for tile in tiles[slot]]
+            weight = weights[0] if len(weights) == 1 else jnp.concatenate(weights, axis=0)
+            value = values[slot][head * DH : (head + 1) * DH, begin:end]
+            value = jnp.concatenate([value, ones[:, begin:end]], axis=0)
+            term = jnp.dot(value, weight, preferred_element_type=jnp.float32)
+            result = term if result is None else result + term
+        return result[:DH] * (1.0 / result[DH : DH + 1])
 
     ready = score_unit(*units[0])
-    tiles_out = [None] * (WIDE // LANES)
-    for index, (part, window) in enumerate(units):
+    heads = []
+    for index, (part, head) in enumerate(units):
         following = score_unit(*units[index + 1]) if index + 1 < len(units) else None
-        result = value_unit(part, window, *ready)
-        for lane in range(0, window[1], LANES):
-            place = (window[0] + lane) // LANES
-            piece = result[:, lane : lane + LANES]
-            tiles_out[place] = piece if tiles_out[place] is None else tiles_out[place] + piece
-        if window is WINDOWS[-1]:
-            for place, piece in enumerate(tiles_out):
-                out_ref[
-                    part * SUB : (part + 1) * SUB, place * LANES : (place + 1) * LANES
-                ] = piece.astype(out_ref.dtype)
-            tiles_out = [None] * (WIDE // LANES)
+        heads.append(value_unit(part, head, *ready))
+        if head == BUNDLE - 1:
+            result = jnp.concatenate(heads, axis=0).T
+            out_ref[part * SUB : (part + 1) * SUB, :] = result.astype(out_ref.dtype)
+            heads = []
         ready = following
 
 
@@ -253,17 +246,17 @@
     exact_ref, first_ref, sent_ref = rest[-3:]
     rows = key_ref.shape[0]
     lane = lax.broadcasted_iota(jnp.int32, (DH, LANES), 1)
-    key_t = key_ref[...].T
+    value_t = value_ref[...].T
     for head, (start, width, place) in enumerate(WINDOWS):
         lanes = slice(start, start + width)
         state, before = None, None
         for at in range(0, rows, SUB):
-            running = decay_ref[0, at : at + SUB, head : head + 1]
-            anchor = running[SUB - 1 :, :]
-            value = value_ref[at : at + SUB, lanes].astype(jnp.float32) * jnp.exp(anchor - running)
+            running = decay_ref[0, head : head + 1, at : at + SUB]
+            anchor = running[:, SUB - 1 :]
+            value = value_t[head * DH : (head + 1) * DH, at : at + SUB].astype(jnp.float32)
             update = jnp.dot(
-                key_t[head * DH : (head + 1) * DH, at : at + SUB],
-                value.astype(jnp.bfloat16),
+                (value * jnp.exp(anchor - running)).astype(jnp.bfloat16),
+                key_ref[at : at + SUB, lanes],
                 preferred_element_type=jnp.float32,
             )
             if at + SUB == rows:
@@ -284,23 +277,7 @@
     return jnp.where(lane < DH, state, 0.0)
 
 
-def widen(state, width, place):
-    lane = lax.broadcasted_iota(jnp.int32, state.shape, 1)
-    state = jnp.where(lane < DH, state, 0.0)
-    if width > LANES:
-        state = jnp.concatenate([state, jnp.zeros((DH, width - LANES), jnp.float32)], axis=1)
-    if place:
-        state = pltpu.roll(state, place, axis=1)
-    pads = []
-    if place:
-        pads.append(jnp.zeros((place, width), jnp.float32))
-    pads.append(state)
-    if place + DH < width:
-        pads.append(jnp.zeros((width - place - DH, width), jnp.float32))
-    return jnp.concatenate(pads, axis=0).astype(jnp.bfloat16)
-
-
-def local_state(key, value, decay_cols, deps):
+def local_state(key, value, decay_rows, deps):
     rows, width = key.shape
     bundles = width // WIDE
     block = pl.BlockSpec((rows, WIDE), lambda b: (0, b))
@@ -309,7 +286,7 @@
     return pl.pallas_call(
         state_kernel,
         grid=(bundles,),
-        in_specs=[block, block, pl.BlockSpec((1, rows, BUNDLE), lambda b: (b, 0, 0))]
+        in_specs=[block, block, pl.BlockSpec((1, BUNDLE, rows), lambda b: (b, 0, 0))]
         + untouched(deps),
         out_specs=[out, out, out],
         out_shape=[
@@ -320,7 +297,7 @@
         compiler_params=params(),
         cost_estimate=cheap(),
         name="local_state",
-    )(key, value, decay_cols, *deps)
+    )(key, value, decay_rows, *deps)
 
 
 def chip_state_kernel(info, exact_ref, other_ref, *rest):
@@ -335,18 +312,17 @@
 def chip_state(info, exact, other, deps):
     half = exact.shape[0] // 2
     shape = (half, DH, LANES)
-    block = pl.BlockSpec((BUNDLE, DH, LANES), lambda b, _: (b, 0, 0))
-    steps = half // BUNDLE
+    block = pl.BlockSpec(shape, lambda b, _: (0, 0, 0))
 
     def mine(b, info):
-        return (lax.rem(info[0], 2) * steps + b, 0, 0)
+        return (lax.rem(info[0], 2), 0, 0)
 
     return pl.pallas_call(
         chip_state_kernel,
         grid_spec=pltpu.PrefetchScalarGridSpec(
             num_scalar_prefetch=1,
-            grid=(steps,),
-            in_specs=[pl.BlockSpec((BUNDLE, DH, LANES), mine)] * 2 + untouched(deps),
+            grid=(1,),
+            in_specs=[pl.BlockSpec(shape, mine)] * 2 + untouched(deps),
             out_specs=[block, block],
         ),
         out_shape=[
@@ -373,10 +349,10 @@
 
 
 def join(chip, before, arrived, start, last, deps):
-    block = pl.BlockSpec((BUNDLE, DH, LANES), lambda b: (b, 0, 0))
+    block = pl.BlockSpec(chip.shape, lambda b: (0, 0, 0))
     return pl.pallas_call(
         functools.partial(join_kernel, start, last),
-        grid=(chip.shape[0] // BUNDLE,),
+        grid=(1,),
         in_specs=[block] * 3 + untouched(deps),
         out_specs=[block] * 3,
         out_shape=[
@@ -390,45 +366,39 @@
     )(chip, before, arrived, *deps)
 
 
-def spread(result, start, tiles_out):
-    for lane in range(0, result.shape[1], LANES):
-        tile = (start + lane) // LANES
-        piece = result[:, lane : lane + LANES]
-        tiles_out[tile] = piece if tiles_out[tile] is None else tiles_out[tile] + piece
-
-
 def mix_local_kernel(query_ref, key_ref, value_ref, col_ref, row_ref, first_ref, *rest):
     out_ref = rest[-1]
     rows = query_ref.shape[0]
-    row = lax.broadcasted_iota(jnp.int32, (SUB, SUB), 0)
-    col = lax.broadcasted_iota(jnp.int32, (SUB, SUB), 1)
-    causal = col <= row
+    key_at = lax.broadcasted_iota(jnp.int32, (SUB, SUB), 0)
+    query_at = lax.broadcasted_iota(jnp.int32, (SUB, SUB), 1)
+    causal = key_at <= query_at
+    value_t, query_t = value_ref[...].T, query_ref[...].T
     for at in range(0, rows, SUB):
         here = slice(at, at + SUB)
-        tiles_out = [None] * (WIDE // LANES)
         for head, (start, width, place) in enumerate(WINDOWS):
             lanes = slice(start, start + width)
+            features = slice(head * DH, (head + 1) * DH)
             query = query_ref[here, lanes]
             query = jnp.where(head_lanes(query.shape, place), query, jnp.zeros_like(query))
-            down = col_ref[0, here, head : head + 1]
             score = lax.dot_general(
+                key_ref[here, lanes],
                 query,
-                key_ref[here, lanes],
                 (((1,), (1,)), ((), ())),
                 preferred_element_type=jnp.float32,
             )
-            gap = jnp.where(causal, down - row_ref[0, head : head + 1, here], -jnp.inf)
+            along = row_ref[0, head : head + 1, here]
+            gap = jnp.where(causal, along - col_ref[0, here, head : head + 1], -jnp.inf)
             mixing = (score * jnp.exp(gap)).astype(jnp.bfloat16)
-            result = jnp.dot(mixing, value_ref[here, lanes], preferred_element_type=jnp.float32)
+            result = jnp.dot(value_t[features, here], mixing, preferred_element_type=jnp.float32)
             if at:
-                since = down - col_ref[0, at - 1 : at, head : head + 1]
-                scaled = (query.astype(jnp.float32) * jnp.exp(since)).astype(jnp.bfloat16)
+                since = along - row_ref[0, head : head + 1, at - 1 : at]
+                scaled = query_t[features, here].astype(jnp.float32) * jnp.exp(since)
                 result = result + jnp.dot(
-                    scaled, widen(first_ref[head], width, place), preferred_element_type=jnp.float32
+                    first_ref[head][:, :DH].astype(jnp.bfloat16),
+                    scaled.astype(jnp.bfloat16),
+                    preferred_element_type=jnp.float32,
                 )
-            spread(jnp.where(head_lanes(result.shape, place), result, 0.0), start, tiles_out)
-        for tile, piece in enumerate(tiles_out):
-            out_ref[here, tile * LANES : (tile + 1) * LANES] = piece
+            out_ref[features, here] = result
 
 
 def mix_local(query, key, value, decay_cols, decay_rows, first, deps):
@@ -446,41 +416,36 @@
             pl.BlockSpec((BUNDLE, DH, LANES), lambda b: (b, 0, 0)),
         ]
         + untouched(deps),
-        out_specs=block,
-        out_shape=jax.ShapeDtypeStruct((rows, width), jnp.float32),
+        out_specs=pl.BlockSpec((WIDE, rows), lambda b: (b, 0)),
+        out_shape=jax.ShapeDtypeStruct((width, rows), jnp.float32),
         compiler_params=params(),
         cost_estimate=cheap(),
         name="mix_local",
     )(query, key, value, decay_cols, decay_rows, first, *deps)
 
 
-def mix_final_kernel(half, info, query_ref, local_ref, col_ref, own_ref, sent_ref, other_ref, *rest):
+def mix_final_kernel(half, info, query_ref, local_ref, row_ref, own_ref, sent_ref, other_ref, *rest):
     out_ref = rest[-1]
-    rows = query_ref.shape[0]
     core = lax.rem(info[0], 2)
     mine = (pl.program_id(0) >= half).astype(jnp.int32) == core
-    states = []
-    for head, (_, width, place) in enumerate(WINDOWS):
+    query_t = query_ref[...].T
+    heads = []
+    for head in range(BUNDLE):
+        features = slice(head * DH, (head + 1) * DH)
         state = jnp.where(mine, own_ref[head], opened(sent_ref[head]))
         state = jnp.where(core == 0, state, joined(state, opened(other_ref[head])))
-        states.append(widen(state, width, place))
-    for at in range(0, rows, SUB):
-        here = slice(at, at + SUB)
-        tiles_out = [None] * (WIDE // LANES)
-        for head, (start, width, place) in enumerate(WINDOWS):
-            lanes = slice(start, start + width)
-            inside = head_lanes((SUB, width), place)
-            query = jnp.where(inside, query_ref[here, lanes].astype(jnp.float32), 0.0)
-            scaled = (query * jnp.exp(col_ref[0, here, head : head + 1])).astype(jnp.bfloat16)
-            result = jnp.dot(scaled, states[head], preferred_element_type=jnp.float32)
-            result = jnp.where(inside, result + local_ref[here, lanes], 0.0)
-            square = jnp.sum(result * result, axis=1, keepdims=True) * (1.0 / DH)
-            spread(result * lax.rsqrt(square + EPS_NORM), start, tiles_out)
-        for tile, piece in enumerate(tiles_out):
-            out_ref[here, tile * LANES : (tile + 1) * LANES] = piece.astype(out_ref.dtype)
-
-
-def mix_final(info, query, local, decay_cols, own, sent, other, deps):
+        scaled = query_t[features, :].astype(jnp.float32) * jnp.exp(row_ref[0, head : head + 1, :])
+        result = local_ref[features, :] + jnp.dot(
+            state[:, :DH].astype(jnp.bfloat16),
+            scaled.astype(jnp.bfloat16),
+            preferred_element_type=jnp.float32,
+        )
+        square = jnp.sum(result * result, axis=0, keepdims=True) * (1.0 / DH)
+        heads.append(result * lax.rsqrt(square + EPS_NORM))
+    out_ref[...] = jnp.concatenate(heads, axis=0).T.astype(out_ref.dtype)
+
+
+def mix_final(info, query, local, decay_rows, own, sent, other, deps):
     rows, width = query.shape
     bundles = width // WIDE
     half = bundles // 2
@@ -494,8 +459,8 @@
             grid=(bundles,),
             in_specs=[
                 block,
-                block,
-                pl.BlockSpec((1, rows, BUNDLE), lambda b, _: (b, 0, 0)),
+                pl.BlockSpec((WIDE, rows), lambda b, _: (b, 0)),
+                pl.BlockSpec((1, BUNDLE, rows), lambda b, _: (b, 0, 0)),
                 halves,
                 halves,
                 states,
@@ -507,12 +472,12 @@
         compiler_params=params(),
         cost_estimate=cheap(),
         name="mix_final",
-    )(info, query, local, decay_cols, own, sent, other, *deps)
+    )(info, query, local, decay_rows, own, sent, other, *deps)
 
 
 def group_sizes(bundles):
     if bundles == 8:
-        return [2, 3, 2, 1]
+        return [2, 2, 3, 1]
     return [1] * bundles
 
 
@@ -548,6 +513,7 @@
     def do_back(group):
         if group < groups:
             near[group] = gate(near[group], done["last"])
+            done["last"] = [near[group]]
             back[group] = moved(near[group], back_pairs)
 
     def do_pick(group):
@@ -570,7 +536,7 @@
         running = jnp.cumsum(log_decay, axis=0)
         light["cols"] = running.reshape(rows, bundles, BUNDLE).transpose(1, 0, 2)
         light["rows"] = running.T.reshape(bundles, BUNDLE, rows)
-        exact, first, sent = local_state(key1, value1, light["cols"], done["last"])
+        exact, first, sent = local_state(key1, value1, light["rows"], done["last"])
         light["first"] = first
         light["other"] = moved(sent, swap_pairs)
         light["exact"] = exact
@@ -605,7 +571,7 @@
         while light["distance"] < count // 2:
             do_join()
         light["normed"] = mix_final(
-            info, query1, light["local"], light["cols"], light["before"], light["arrived"],
+            info, query1, light["local"], light["rows"], light["before"], light["arrived"],
             light["other"], done["last"],
         )
         done["last"] = [light["normed"]]
@@ -620,30 +586,29 @@
         done["last"] = done["last"] + [chip[group]]
 
     do_pack(0)
+    do_pack(1)
     do_state()
-    do_pack(1)
     do_back(0)
     do_mix_local()
     wait_chip(0)
     do_chip()
+    do_back(1)
     do_pick(0)
     do_join()
     do_attend(0)
     do_join()
-    do_back(1)
-    wait_chip(1)
     do_join()
     do_pack(2)
+    do_pick(1)
     do_mix_final()
-    do_pick(1)
     do_project()
     do_back(2)
     do_pack(3)
     do_attend(1)
     do_back(3)
     do_pick(2)
+    do_attend(2)
     do_pick(3)
-    do_attend(2)
     do_attend(3)
     return (done["linear"], done["attended"])
 

time: 352 us -> 284 us (0.81)
  the two profiles are of different devices: /device:TPU:25 before, /device:TPU:31 now
where the time goes in v2:
time: 284 us; the launch traced here: 279 us
  Pallas kernels  124 us (44%)
  waiting for transfers between devices  57.3 us (20%)
  starting transfers between devices  56.5 us (20%)
  matrix products  15.9 us (6%)
  between operations  14.7 us (5%)
  local copies, waits for them, and re-layouts  8.56 us (3%)
    ppermute x21, waiting for transfers between devices, moved(): lax.ppermute(value, 'ctx', [(s, t) for s, t in pairs if 0 <= t < count])  57.3 us
    ppermute x21, starting transfers between devices, moved(): lax.ppermute(value, 'ctx', [(s, t) for s, t in pairs if 0 <= t < count])  56.5 us
    pallas_call x4, Pallas kernels, attend(): pl.pallas_call(attend_kernel, grid_spec=pltpu.PrefetchScalarGridSpec(num_...  51.7 us
    dot_general x1, matrix products, do_project(): jnp.dot(light['normed'], out_weight, preferred_element_type=jnp.float32)  15.9 us
    pallas_call x4, Pallas kernels, pick(): pl.pallas_call(pick_kernel, grid_spec=pltpu.PrefetchScalarGridSpec(num_sc...  14.8 us
    pallas_call x1, Pallas kernels, mix_local(): pl.pallas_call(mix_local_kernel, grid=(width // WIDE,), in_specs=[block,...  14.3 us
    pallas_call x1, Pallas kernels, mix_final(): pl.pallas_call(functools.partial(mix_final_kernel, half), grid_spec=pltpu...  11.3 us
    pallas_call x4, Pallas kernels, pack(): pl.pallas_call(pack_kernel, grid=(bundles,), in_specs=[block, block] + un...  10.9 us
  transfers between devices with their start and end apart: 22, of which 5 were waited for; matrix products, arithmetic and copies ran while one was open for 7% of the time, Pallas kernels for 42%

profile of v2, /device:TPU:31, one launch (start us, length us, event | category | flops | bytes accessed | tf_op | source)
XLA Modules:
  0.0 278.8 jit_solution(5592898762104740100)
XLA Ops:
  7.2 0.0 copy-start
  7.2 0.0 reduce-scatter.2.cloned.1.call-start
  7.2 2.3 pack.4.rest_0_
  9.6 1.3 collective-permute-start
  10.9 1.3 collective-permute-start.2
  12.2 2.4 pack.5.rest_0_
  14.5 1.3 collective-permute-start.5
  15.8 1.2 reduce-window.6
  17.0 0.2 slice_reduce_fusion
  17.2 0.1 broadcast_add_fusion
  17.3 0.7 reduce_window_sum.21.decay_ref.row_ref
  18.0 9.3 %local_state.1 = (f32[32,96,128]{2,1,0:T(8,128)}, f32[32,96,128]{2,1,0:T(8,128)}, bf16[32,96,128]{2,1,0:T(8,128)(2,1)}) custom-call(bf16[512,3072]{1,0:T(8,128)(2,1)} %key_ref.13, bf16[512,3072]{1,0:T(8,128)(2,1)} %value_ref.13, f32[8,4,512]{2,1,0:T(4,128)} %reduce_window_sum.21.decay_ref.row_ref, bf16[2,512,768]{2,1,0:T(8,128)(2,1)} %pack.5.rest_0_), custom_call_target="tpu_custom_call" | custom-call | flops 1000 | bytes 1000 | tf_op jit(solution)/shard_map/local_state/pallas_call | solution.py:286
  27.3 1.8 collective-permute-start.4
  29.1 19.9 %collective-permute-start.1 = (bf16[32,96,128]{2,1,0:T(8,128)(2,1)}, bf16[32,96,128]{2,1,0:T(8,128)(2,1)S(1)}, u32[]{:S(2)}, u32[]{:S(2)}) collective-permute-start(bf16[32,96,128]{2,1,0:T(8,128)(2,1)} %get-tuple-element.16.refs_1_), channel_id=1, source_target_pairs={{0,2},{2,0},{4,6},{6,4},{8,10},{10,8},{12,14},{14,12},{16,18},{18,... | collective-permute-start | bytes 2359304 | tf_op jit(solution)/shard_map/ppermute | solution.py:492
  49.0 0.1 bitcast_bitcast_fusion
  49.2 2.0 copy.21
  51.1 14.3 %mix_local.1.rest_0_.local_ref = f32[3072,512]{1,0:T(8,128)} custom-call(bf16[512,3072]{1,0:T(8,128)(2,1)} %query_ref.8, bf16[512,3072]{1,0:T(8,128)(2,1)} %key_ref.13, bf16[512,3072]{1,0:T(8,128)(2,1)} %value_ref.13, f32[8,512,4]{2,1,0:T(8,128)} %bitcast.19, f32[8,4,512]{2,1,0:T(4,128)} %reduce_window_sum.21.decay_ref.row_ref, ...), custom_call_target="tpu_custom_call" | custom-call | flops 1000 | bytes 1000 | tf_op jit(solution)/shard_map/mix_local/pallas_call | solution.py:407
  65.4 0.0 collective-permute-done.1.other_ref
  65.5 0.9 copy-done.4
  66.3 2.7 chip_state.1
  69.0 0.0 collective-permute-done.4.back_ref
  69.0 3.8 %pick.4.rest_0_.mid_ref = bf16[2,512,768]{2,1,0:T(8,128)(2,1)} custom-call(s32[1]{0:T(128)} %bitcast.info, bf16[2,512,768]{2,1,0:T(8,128)(2,1)} %collective-permute-done.2.rest_1_.chip_ref, bf16[2,512,768]{2,1,0:T(8,128)(2,1)} %collective-permute-done.4.back_ref, bf16[2,512,768]{2,1,0:T(8,128)(2,1)} %gate.5.rest_0_.near_ref), custom_call_target="tpu_custom_call" | custom-call | flops 1000 | bytes 1000 | tf_op jit(solution)/shard_map/pick/pallas_call | solution.py:101
  72.8 1.3 collective-permute-start.3
  74.1 1.3 collective-permute-start.10
  75.4 1.8 collective-permute-start.11
  77.3 7.6 %collective-permute-done.3.arrived_ref = bf16[16,96,128]{2,1,0:T(8,128)(2,1)S(1)} collective-permute-done((bf16[16,96,128]{2,1,0:T(8,128)(2,1)S(1)}, bf16[16,96,128]{2,1,0:T(8,128)(2,1)S(1)}, u32[]{:S(2)}, u32[]{:S(2)}) %collective-permute-start.3) | collective-permute-done | bytes 393248 | tf_op jit(solution)/shard_map/ppermute | solution.py:492
  84.9 0.8 copy-done.7
  85.7 3.3 %join.3 = (f32[16,96,128]{2,1,0:T(8,128)}, f32[16,96,128]{2,1,0:T(8,128)}, bf16[16,96,128]{2,1,0:T(8,128)(2,1)}) custom-call(f32[16,96,128]{2,1,0:T(8,128)} %get-tuple-element.18.chip_ref.before_ref, f32[16,96,128]{2,1,0:T(8,128)} %get-tuple-element.18.chip_ref.before_ref, bf16[16,96,128]{2,1,0:T(8,128)(2,1)} %copy-done.7, ...), custom_call_target="tpu_custom_call" | custom-call | flops 1000 | bytes 1000 | tf_op jit(solution)/shard_map/join/pallas_call | solution.py:353
  89.0 1.7 collective-permute-start.6
  90.7 12.9 %attend.4.rest_0_ = bf16[512,3072]{1,0:T(8,128)(2,1)} custom-call(s32[1]{0:T(128)} %bitcast.info, bf16[512,3072]{1,0:T(8,128)(2,1)} %query_ref.11, bf16[512,3072]{1,0:T(8,128)(2,1)} %key_ref.19, bf16[512,3072]{1,0:T(8,128)(2,1)} %value_ref.19, bf16[2,512,768]{2,1,0:T(8,128)(2,1)} %gate.4.rest_0_.near_ref, bf16[2,512,768]{2,1,0:T(8,128)(2,1)} %pick.4.rest_0_.mid_ref, ...), custom_call_target="tpu_custom_call" | custom-call | flops 1000 | bytes 1000 | tf_op jit(solution)/shard_map/attend/pallas_call | solution.py:210
  103.6 0.7 copy-done.8
  104.4 3.1 %join.4 = (f32[16,96,128]{2,1,0:T(8,128)}, f32[16,96,128]{2,1,0:T(8,128)}, bf16[16,96,128]{2,1,0:T(8,128)(2,1)}) custom-call(f32[16,96,128]{2,1,0:T(8,128)} %get-tuple-element.20.chip_ref, f32[16,96,128]{2,1,0:T(8,128)} %get-tuple-element.21.before_ref, bf16[16,96,128]{2,1,0:T(8,128)(2,1)} %copy-done.8, bf16[512,3072]{1,0:T(8,128)(2,1)} %attend.4.rest_0_), custom_call_target="tpu_custom_call" | custom-call | flops 1000 | bytes 1000 | tf_op jit(solution)/shard_map/join/pallas_call | solution.py:353
  107.5 1.3 collective-permute-start.8
  108.8 18.0 %collective-permute-done.8.arrived_ref = bf16[16,96,128]{2,1,0:T(8,128)(2,1)S(1)} collective-permute-done((bf16[16,96,128]{2,1,0:T(8,128)(2,1)}, bf16[16,96,128]{2,1,0:T(8,128)(2,1)S(1)}, u32[]{:S(2)}, u32[]{:S(2)}) %collective-permute-start.8) | collective-permute-done | bytes 393248 | tf_op jit(solution)/shard_map/ppermute | solution.py:492
  126.8 0.7 copy-done.9
  127.6 3.0 %join.5 = (f32[16,96,128]{2,1,0:T(8,128)}, f32[16,96,128]{2,1,0:T(8,128)}, bf16[16,96,128]{2,1,0:T(8,128)(2,1)}) custom-call(f32[16,96,128]{2,1,0:T(8,128)} %get-tuple-element.23.chip_ref, f32[16,96,128]{2,1,0:T(8,128)} %get-tuple-element.24.before_ref, bf16[16,96,128]{2,1,0:T(8,128)(2,1)} %copy-done.9, bf16[16,96,128]{2,1,0:T(8,128)(2,1)} %get-tuple-element.25.rest_0_), custom_call_target="tpu_custom_call" | custom-call | flops 1000 | bytes 1000 | tf_op jit(solution)/shard_map/join/pallas_call | solution.py:353
  130.6 3.6 %collective-permute-start.9 = (bf16[16,96,128]{2,1,0:T(8,128)(2,1)}, bf16[16,96,128]{2,1,0:T(8,128)(2,1)S(1)}, u32[]{:S(2)}, u32[]{:S(2)}) collective-permute-start(bf16[16,96,128]{2,1,0:T(8,128)(2,1)} %get-tuple-element.27.rest_0_), channel_id=1, source_target_pairs={{0,2},{2,0},{4,6},{6,4},{8,10},{10,8},{12,14},{14,12},{16,18},{18,... | collective-permute-start | bytes 1179656 | tf_op jit(solution)/shard_map/ppermute | solution.py:492
  134.2 3.9 %pack.6.rest_0_ = bf16[2,512,1152]{2,1,0:T(8,128)(2,1)} custom-call(bf16[512,3072]{1,0:T(8,128)(2,1)} %key_ref.19, bf16[512,3072]{1,0:T(8,128)(2,1)} %value_ref.19, bf16[16,96,128]{2,1,0:T(8,128)(2,1)} %get-tuple-element.27.rest_0_), custom_call_target="tpu_custom_call" | custom-call | flops 1000 | bytes 1000 | tf_op jit(solution)/shard_map/pack/pallas_call | solution.py:64
  138.1 1.5 collective-permute-start.12
  139.6 0.0 collective-permute-done.11.back_ref
  139.6 3.8 %pick.5.rest_0_.mid_ref = bf16[2,512,768]{2,1,0:T(8,128)(2,1)} custom-call(s32[1]{0:T(128)} %bitcast.info, bf16[2,512,768]{2,1,0:T(8,128)(2,1)} %collective-permute-done.10.chip_ref, bf16[2,512,768]{2,1,0:T(8,128)(2,1)} %collective-permute-done.11.back_ref, bf16[2,512,1152]{2,1,0:T(8,128)(2,1)} %pack.6.rest_0_), custom_call_target="tpu_custom_call" | custom-call | flops 1000 | bytes 1000 | tf_op jit(solution)/shard_map/pick/pallas_call | solution.py:101
  143.4 0.7 copy-done.10
  144.1 11.3 %mix_final.1 = bf16[512,3072]{1,0:T(8,128)(2,1)} custom-call(s32[1]{0:T(128)} %bitcast.info, bf16[512,3072]{1,0:T(8,128)(2,1)} %query_ref.8, f32[3072,512]{1,0:T(8,128)} %mix_local.1.rest_0_.local_ref, f32[8,4,512]{2,1,0:T(4,128)} %reduce_window_sum.21.decay_ref.row_ref, f32[16,96,128]{2,1,0:T(8,128)} %get-tuple-element.26.own_ref, ...), custom_call_target="tpu_custom_call" | custom-call | flops 1000 | bytes 1000 | tf_op jit(solution)/shard_map/mix_final/pallas_call | solution.py:455
  155.5 15.9 %convolution_convert_fusion.refs_1_ = bf16[512,3072]{1,0:T(8,128)(2,1)} fusion(bf16[512,3072]{1,0:T(8,128)(2,1)} %mix_final.1, bf16[3072,3072]{1,0:T(8,128)(2,1)} %param.12), kind=kOutput, calls=%fused_computation | convolution fusion | flops 9665249280 | bytes 25165824 | tf_op jit(solution)/shard_map/dot_general | solution.py:580
  171.3 0.0 reduce-scatter.2.cloned.1.call-update
  171.3 1.3 collective-permute-start.17
  172.7 2.1 collective-permute-start.18
  174.8 5.1 %collective-permute-start.14 = (bf16[2,512,768]{2,1,0:T(8,128)(2,1)}, bf16[2,512,768]{2,1,0:T(8,128)(2,1)}, u32[]{:S(2)}, u32[]{:S(2)}) collective-permute-start(bf16[2,512,768]{2,1,0:T(8,128)(2,1)} %pick.5.rest_0_.mid_ref), channel_id=1, source_target_pairs={{0,2},{2,0},{4,6},{6,4},{8,10},{10,8},{12,14},{14,12},{16,18},{18,... | collective-permute-start | bytes 4718600 | tf_op jit(solution)/shard_map/ppermute | solution.py:492
  179.8 2.2 pack.7.rest_1_
  182.1 1.3 collective-permute-start.13
  183.4 12.9 %attend.5.refs_1_.rest_0_ = bf16[512,3072]{1,0:T(8,128)(2,1)} custom-call(s32[1]{0:T(128)} %bitcast.info, bf16[512,3072]{1,0:T(8,128)(2,1)} %query_ref.11, bf16[512,3072]{1,0:T(8,128)(2,1)} %key_ref.19, bf16[512,3072]{1,0:T(8,128)(2,1)} %value_ref.19, bf16[2,512,768]{2,1,0:T(8,128)(2,1)} %gate.5.rest_0_.near_ref, ...), custom_call_target="tpu_custom_call", output_to_operand_aliasing={{}: (7, {})} | custom-call | flops 1000 | bytes 1000 | tf_op jit(solution)/shard_map/attend/pallas_call | solution.py:210
  196.3 0.9 copy-done.2
  197.2 28.0 %collective-permute-done.17.chip_ref = bf16[2,512,1152]{2,1,0:T(8,128)(2,1)} collective-permute-done((bf16[2,512,1152]{2,1,0:T(8,128)(2,1)}, bf16[2,512,1152]{2,1,0:T(8,128)(2,1)}, u32[]{:S(2)}, u32[]{:S(2)}) %collective-permute-start.17) | collective-permute-done | bytes 2359328 | tf_op jit(solution)/shard_map/ppermute | solution.py:492
  225.2 5.1 %pick.6.mid_ref.rest_1_ = bf16[2,512,1152]{2,1,0:T(8,128)(2,1)} custom-call(s32[1]{0:T(128)} %bitcast.info, bf16[2,512,1152]{2,1,0:T(8,128)(2,1)} %collective-permute-done.17.chip_ref, bf16[2,512,1152]{2,1,0:T(8,128)(2,1)} %collective-permute-done.18.back_ref, bf16[2,512,384]{2,1,0:T(8,128)(2,1)} %gate.7.rest_0_.near_ref), custom_call_target="tpu_custom_call" | custom-call | flops 1000 | bytes 1000 | tf_op jit(solution)/shard_map/pick/pallas_call | solution.py:101
  230.3 2.4 collective-permute-start.19
  232.7 1.3 collective-permute-start.15
  234.0 1.7 collective-permute-start.16
  235.8 1.5 collective-permute-done.19.swap_ref
  237.3 17.9 %attend.6.rest_0_ = bf16[512,3072]{1,0:T(8,128)(2,1)} custom-call(s32[1]{0:T(128)} %bitcast.info, bf16[512,3072]{1,0:T(8,128)(2,1)} %query_ref.11, bf16[512,3072]{1,0:T(8,128)(2,1)} %key_ref.19, bf16[512,3072]{1,0:T(8,128)(2,1)} %value_ref.19, bf16[2,512,1152]{2,1,0:T(8,128)(2,1)} %gate.6.rest_0_.near_ref, ...), custom_call_target="tpu_custom_call", output_to_operand_aliasing={{}: (7, {})} | custom-call | flops 1000 | bytes 1000 | tf_op jit(solution)/shard_map/attend/pallas_call | solution.py:210
  255.2 2.1 pick.7.mid_ref.rest_1_
  257.3 3.2 %collective-permute-start.20 = (bf16[2,512,384]{2,1,0:T(8,128)(2,1)}, bf16[2,512,384]{2,1,0:T(8,128)(2,1)S(1)}, u32[]{:S(2)}, u32[]{:S(2)}) collective-permute-start(bf16[2,512,384]{2,1,0:T(8,128)(2,1)} %pick.7.mid_ref.rest_1_), channel_id=1, source_target_pairs={{0,2},{2,0},{4,6},{6,4},{8,10},{10,8},{12,14},{14,12},{16,18},{18,... | collective-permute-start | bytes 2359304 | tf_op jit(solution)/shard_map/ppermute | solution.py:492
  260.4 2.1 collective-permute-done.20.swap_ref
  262.6 0.9 copy-done.5
  263.5 8.0 %attend.7 = bf16[512,3072]{1,0:T(8,128)(2,1)} custom-call(s32[1]{0:T(128)} %bitcast.info, bf16[512,3072]{1,0:T(8,128)(2,1)} %query_ref.11, bf16[512,3072]{1,0:T(8,128)(2,1)} %key_ref.19, bf16[512,3072]{1,0:T(8,128)(2,1)} %value_ref.19, bf16[2,512,384]{2,1,0:T(8,128)(2,1)} %gate.7.rest_0_.near_ref, ...), custom_call_target="tpu_custom_call", output_to_operand_aliasing={{}: (7, {})} | custom-call | flops 1000 | bytes 1000 | tf_op jit(solution)/shard_map/attend/pallas_call | solution.py:210
  (38 shorter events, 0.2 us)
Async XLA Ops:
  7.2 8.6 %copy-start = (f32[512,32]{0,1:T(8,128)S(1)}, f32[512,32]{0,1:T(8,128)}, u32[]{:S(2)}) copy-start(f32[512,32]{0,1:T(8,128)} %param.11) | copy-start | bytes 196612
  7.2 264.3 %reduce-scatter.2.cloned.1.call-start = ((), (), s32[]{:S(2)}) async-start(), calls=%async_computation.1 | async-start | bytes 4718592 | tf_op jit(solution)/shard_map/reduce_scatter | solution.py:582
  9.6 17.8 %collective-permute-start = (bf16[2,512,768]{2,1,0:T(8,128)(2,1)}, bf16[2,512,768]{2,1,0:T(8,128)(2,1)}, u32[]{:S(2)}, u32[]{:S(2)}) collective-permute-start(bf16[2,512,768]{2,1,0:T(8,128)(2,1)} %pack.4.rest_0_), channel_id=1, source_target_pairs={{0,2},{2,8},{4,6},{6,12},{8,10},{10,16},{12,14},{14,20},{16,18},{1... | collective-permute-start | bytes 4718600 | tf_op jit(solution)/shard_map/ppermute | solution.py:492
  10.9 54.6 %collective-permute-start.2 = (bf16[2,512,768]{2,1,0:T(8,128)(2,1)}, bf16[2,512,768]{2,1,0:T(8,128)(2,1)}, u32[]{:S(2)}, u32[]{:S(2)}) collective-permute-start(bf16[2,512,768]{2,1,0:T(8,128)(2,1)} %pack.4.rest_0_), channel_id=1, source_target_pairs={{0,4},{2,6},{4,8},{8,12},{10,14},{12,16},{16,20},{18,22},{20,24},{... | collective-permute-start | bytes 4718600 | tf_op jit(solution)/shard_map/ppermute | solution.py:492
  14.5 54.5 %collective-permute-start.5 = (bf16[2,512,768]{2,1,0:T(8,128)(2,1)}, bf16[2,512,768]{2,1,0:T(8,128)(2,1)}, u32[]{:S(2)}, u32[]{:S(2)}) collective-permute-start(bf16[2,512,768]{2,1,0:T(8,128)(2,1)} %pack.5.rest_0_), channel_id=1, source_target_pairs={{0,2},{2,8},{4,6},{6,12},{8,10},{10,16},{12,14},{14,20},{16,18},{1... | collective-permute-start | bytes 4718600 | tf_op jit(solution)/shard_map/ppermute | solution.py:492
  27.3 41.7 %collective-permute-start.4 = (bf16[2,512,768]{2,1,0:T(8,128)(2,1)}, bf16[2,512,768]{2,1,0:T(8,128)(2,1)}, u32[]{:S(2)}, u32[]{:S(2)}) collective-permute-start(bf16[2,512,768]{2,1,0:T(8,128)(2,1)} %gate.4.rest_0_.near_ref), channel_id=1, source_target_pairs={{12,10},{20,18},{28,26},{13,11},{21,19},{29,27}} | collective-permute-start | bytes 4718600 | tf_op jit(solution)/shard_map/ppermute | solution.py:492
  29.1 36.3 %collective-permute-start.1 = (bf16[32,96,128]{2,1,0:T(8,128)(2,1)}, bf16[32,96,128]{2,1,0:T(8,128)(2,1)S(1)}, u32[]{:S(2)}, u32[]{:S(2)}) collective-permute-start(bf16[32,96,128]{2,1,0:T(8,128)(2,1)} %get-tuple-element.16.refs_1_), channel_id=1, source_target_pairs={{0,2},{2,0},{4,6},{6,4},{8,10},{10,8},{12,14},{14,12},{16,18},{18,... | collective-permute-start | bytes 2359304 | tf_op jit(solution)/shard_map/ppermute | solution.py:492
  65.4 0.9 copy-start.4
  69.0 3.8 %copy-start.6 = (bf16[16,96,128]{2,1,0:T(8,128)(2,1)S(1)}, bf16[16,96,128]{2,1,0:T(8,128)(2,1)}, u32[]{:S(2)}) copy-start(bf16[16,96,128]{2,1,0:T(8,128)(2,1)} %get-tuple-element.19.refs_1_) | copy-start | bytes 1179652
  72.8 17.9 %collective-permute-start.7 = (bf16[2,512,768]{2,1,0:T(8,128)(2,1)}, bf16[2,512,768]{2,1,0:T(8,128)(2,1)}, u32[]{:S(2)}, u32[]{:S(2)}) collective-permute-start(bf16[2,512,768]{2,1,0:T(8,128)(2,1)} %pick.4.rest_0_.mid_ref), channel_id=1, source_target_pairs={{0,2},{2,0},{4,6},{6,4},{8,10},{10,8},{12,14},{14,12},{16,18},{18,... | collective-permute-start | bytes 4718600 | tf_op jit(solution)/shard_map/ppermute | solution.py:492
  72.8 12.1 %collective-permute-start.3 = (bf16[16,96,128]{2,1,0:T(8,128)(2,1)S(1)}, bf16[16,96,128]{2,1,0:T(8,128)(2,1)S(1)}, u32[]{:S(2)}, u32[]{:S(2)}) collective-permute-start(bf16[16,96,128]{2,1,0:T(8,128)(2,1)S(1)} %copy-done.6), channel_id=1, source_target_pairs={{0,4},{2,6},{4,8},{6,10},{8,12},{10,14},{12,16},{14,18},{16,20},{1... | collective-permute-start | bytes 1179656 | tf_op jit(solution)/shard_map/ppermute | solution.py:492
  74.1 65.4 %collective-permute-start.10 = (bf16[2,512,768]{2,1,0:T(8,128)(2,1)}, bf16[2,512,768]{2,1,0:T(8,128)(2,1)}, u32[]{:S(2)}, u32[]{:S(2)}) collective-permute-start(bf16[2,512,768]{2,1,0:T(8,128)(2,1)} %pack.5.rest_0_), channel_id=1, source_target_pairs={{0,4},{2,6},{4,8},{8,12},{10,14},{12,16},{16,20},{18,22},{20,24},{... | collective-permute-start | bytes 4718600 | tf_op jit(solution)/shard_map/ppermute | solution.py:492
  75.4 64.2 %collective-permute-start.11 = (bf16[2,512,768]{2,1,0:T(8,128)(2,1)}, bf16[2,512,768]{2,1,0:T(8,128)(2,1)}, u32[]{:S(2)}, u32[]{:S(2)}) collective-permute-start(bf16[2,512,768]{2,1,0:T(8,128)(2,1)} %gate.5.rest_0_.near_ref), channel_id=1, source_target_pairs={{12,10},{20,18},{28,26},{13,11},{21,19},{29,27}} | collective-permute-start | bytes 4718600 | tf_op jit(solution)/shard_map/ppermute | solution.py:492
  84.9 0.8 copy-start.7
  89.0 14.6 %collective-permute-start.6 = (bf16[16,96,128]{2,1,0:T(8,128)(2,1)}, bf16[16,96,128]{2,1,0:T(8,128)(2,1)S(1)}, u32[]{:S(2)}, u32[]{:S(2)}) collective-permute-start(bf16[16,96,128]{2,1,0:T(8,128)(2,1)} %get-tuple-element.22.rest_0_), channel_id=1, source_target_pairs={{0,8},{2,10},{4,12},{6,14},{8,16},{10,18},{12,20},{14,22},{16,24},... | collective-permute-start | bytes 1179656 | tf_op jit(solution)/shard_map/ppermute | solution.py:492
  103.6 0.8 copy-start.8
  107.5 19.3 %collective-permute-start.8 = (bf16[16,96,128]{2,1,0:T(8,128)(2,1)}, bf16[16,96,128]{2,1,0:T(8,128)(2,1)S(1)}, u32[]{:S(2)}, u32[]{:S(2)}) collective-permute-start(bf16[16,96,128]{2,1,0:T(8,128)(2,1)} %get-tuple-element.25.rest_0_), channel_id=1, source_target_pairs={{0,16},{2,18},{4,20},{6,22},{8,24},{10,26},{12,28},{14,30},{1,17},... | collective-permute-start | bytes 1179656 | tf_op jit(solution)/shard_map/ppermute | solution.py:492
  126.8 0.7 copy-start.9
  130.6 12.8 %collective-permute-start.9 = (bf16[16,96,128]{2,1,0:T(8,128)(2,1)}, bf16[16,96,128]{2,1,0:T(8,128)(2,1)S(1)}, u32[]{:S(2)}, u32[]{:S(2)}) collective-permute-start(bf16[16,96,128]{2,1,0:T(8,128)(2,1)} %get-tuple-element.27.rest_0_), channel_id=1, source_target_pairs={{0,2},{2,0},{4,6},{6,4},{8,10},{10,8},{12,14},{14,12},{16,18},{18,... | collective-permute-start | bytes 1179656 | tf_op jit(solution)/shard_map/ppermute | solution.py:492
  138.1 34.5 %collective-permute-start.12 = (bf16[2,512,1152]{2,1,0:T(8,128)(2,1)}, bf16[2,512,1152]{2,1,0:T(8,128)(2,1)}, u32[]{:S(2)}, u32[]{:S(2)}) collective-permute-start(bf16[2,512,1152]{2,1,0:T(8,128)(2,1)} %pack.6.rest_0_), channel_id=1, source_target_pairs={{0,2},{2,8},{4,6},{6,12},{8,10},{10,16},{12,14},{14,20},{16,18},{1... | collective-permute-start | bytes 7077896 | tf_op jit(solution)/shard_map/ppermute | solution.py:492
  143.4 0.7 copy-start.10
  171.3 53.8 %collective-permute-start.17 = (bf16[2,512,1152]{2,1,0:T(8,128)(2,1)}, bf16[2,512,1152]{2,1,0:T(8,128)(2,1)}, u32[]{:S(2)}, u32[]{:S(2)}) collective-permute-start(bf16[2,512,1152]{2,1,0:T(8,128)(2,1)} %pack.6.rest_0_), channel_id=1, source_target_pairs={{0,4},{2,6},{4,8},{8,12},{10,14},{12,16},{16,20},{18,22},{20,24},{... | collective-permute-start | bytes 7077896 | tf_op jit(solution)/shard_map/ppermute | solution.py:492
  172.7 52.5 %collective-permute-start.18 = (bf16[2,512,1152]{2,1,0:T(8,128)(2,1)}, bf16[2,512,1152]{2,1,0:T(8,128)(2,1)}, u32[]{:S(2)}, u32[]{:S(2)}) collective-permute-start(bf16[2,512,1152]{2,1,0:T(8,128)(2,1)} %gate.6.rest_0_.near_ref), channel_id=1, source_target_pairs={{12,10},{20,18},{28,26},{13,11},{21,19},{29,27}} | collective-permute-start | bytes 7077896 | tf_op jit(solution)/shard_map/ppermute | solution.py:492
  174.8 8.6 %collective-permute-start.14 = (bf16[2,512,768]{2,1,0:T(8,128)(2,1)}, bf16[2,512,768]{2,1,0:T(8,128)(2,1)}, u32[]{:S(2)}, u32[]{:S(2)}) collective-permute-start(bf16[2,512,768]{2,1,0:T(8,128)(2,1)} %pick.5.rest_0_.mid_ref), channel_id=1, source_target_pairs={{0,2},{2,0},{4,6},{6,4},{8,10},{10,8},{12,14},{14,12},{16,18},{18,... | collective-permute-start | bytes 4718600 | tf_op jit(solution)/shard_map/ppermute | solution.py:492
  182.1 14.2 %collective-permute-start.13 = (bf16[2,512,384]{2,1,0:T(8,128)(2,1)}, bf16[2,512,384]{2,1,0:T(8,128)(2,1)S(1)}, u32[]{:S(2)}, u32[]{:S(2)}) collective-permute-start(bf16[2,512,384]{2,1,0:T(8,128)(2,1)} %pack.7.rest_1_), channel_id=1, source_target_pairs={{0,2},{2,8},{4,6},{6,12},{8,10},{10,16},{12,14},{14,20},{16,18},{1... | collective-permute-start | bytes 2359304 | tf_op jit(solution)/shard_map/ppermute | solution.py:492
  196.3 0.9 copy-start.2
  197.2 36.9 %copy-start.3 = (bf16[2,512,384]{2,1,0:T(8,128)(2,1)S(1)}, bf16[2,512,384]{2,1,0:T(8,128)(2,1)}, u32[]{:S(2)}) copy-start(bf16[2,512,384]{2,1,0:T(8,128)(2,1)} %gate.7.rest_0_.near_ref) | copy-start | bytes 2359300
  230.3 6.9 %collective-permute-start.19 = (bf16[2,512,1152]{2,1,0:T(8,128)(2,1)}, bf16[2,512,1152]{2,1,0:T(8,128)(2,1)}, u32[]{:S(2)}, u32[]{:S(2)}) collective-permute-start(bf16[2,512,1152]{2,1,0:T(8,128)(2,1)} %pick.6.mid_ref.rest_1_), channel_id=1, source_target_pairs={{0,2},{2,0},{4,6},{6,4},{8,10},{10,8},{12,14},{14,12},{16,18},{18,... | collective-permute-start | bytes 7077896 | tf_op jit(solution)/shard_map/ppermute | solution.py:492
  232.7 22.5 %collective-permute-start.15 = (bf16[2,512,384]{2,1,0:T(8,128)(2,1)}, bf16[2,512,384]{2,1,0:T(8,128)(2,1)}, u32[]{:S(2)}, u32[]{:S(2)}) collective-permute-start(bf16[2,512,384]{2,1,0:T(8,128)(2,1)} %pack.7.rest_1_), channel_id=1, source_target_pairs={{0,4},{2,6},{4,8},{8,12},{10,14},{12,16},{16,20},{18,22},{20,24},{... | collective-permute-start | bytes 2359304 | tf_op jit(solution)/shard_map/ppermute | solution.py:492
  234.0 21.2 %collective-permute-start.16 = (bf16[2,512,384]{2,1,0:T(8,128)(2,1)S(1)}, bf16[2,512,384]{2,1,0:T(8,128)(2,1)}, u32[]{:S(2)}, u32[]{:S(2)}) collective-permute-start(bf16[2,512,384]{2,1,0:T(8,128)(2,1)S(1)} %copy-done.3), channel_id=1, source_target_pairs={{12,10},{20,18},{28,26},{13,11},{21,19},{29,27}} | collective-permute-start | bytes 2359304 | tf_op jit(solution)/shard_map/ppermute | solution.py:492
  257.3 5.3 %collective-permute-start.20 = (bf16[2,512,384]{2,1,0:T(8,128)(2,1)}, bf16[2,512,384]{2,1,0:T(8,128)(2,1)S(1)}, u32[]{:S(2)}, u32[]{:S(2)}) collective-permute-start(bf16[2,512,384]{2,1,0:T(8,128)(2,1)} %pick.7.mid_ref.rest_1_), channel_id=1, source_target_pairs={{0,2},{2,0},{4,6},{6,4},{8,10},{10,8},{12,14},{14,12},{16,18},{18,... | collective-permute-start | bytes 2359304 | tf_op jit(solution)/shard_map/ppermute | solution.py:492
  262.6 0.9 copy-start.5
  263.5 8.0 %copy-start.1 = (f32[512,32]{0,1:T(8,128)S(1)}, f32[512,32]{0,1:T(8,128)}, u32[]{:S(2)}) copy-start(f32[512,32]{0,1:T(8,128)} %param.11) | copy-start | bytes 196612
Sparse Core Ops, SparseCore 0:
  171.5 43.7 reduce-scatter.1

commit v3 on v2

--- a/solution.py
+++ b/solution.py
@@ -477,7 +477,7 @@
 
 def group_sizes(bundles):
     if bundles == 8:
-        return [2, 2, 3, 1]
+        return [2, 3, 2, 1]
     return [1] * bundles
 
 
@@ -526,7 +526,8 @@
         if group < groups:
             done["attended"] = attend(
                 info, query2, key2, value2, near[group], mid[group], swap[group],
-                done["attended"], bases[group], done["last"],
+                done["attended"], bases[group],
+                [array for array in done["last"] if array is not done["attended"]],
             )
             done["last"] = [done["attended"]]
 
@@ -583,32 +584,35 @@
         done["last"] = [product]
 
     def wait_chip(group):
-        done["last"] = done["last"] + [chip[group]]
+        if group < groups:
+            done["last"] = done["last"] + [chip[group]]
 
     do_pack(0)
     do_pack(1)
     do_state()
+    do_mix_local()
     do_back(0)
-    do_mix_local()
     wait_chip(0)
     do_chip()
-    do_back(1)
     do_pick(0)
     do_join()
+    do_back(1)
     do_attend(0)
-    do_join()
+    wait_chip(1)
     do_join()
     do_pack(2)
     do_pick(1)
+    do_join()
+    do_pack(3)
+    wait_chip(2)
     do_mix_final()
+    do_back(2)
     do_project()
-    do_back(2)
-    do_pack(3)
-    do_attend(1)
     do_back(3)
     do_pick(2)
+    do_attend(1)
+    do_pick(3)
     do_attend(2)
-    do_pick(3)
     do_attend(3)
     return (done["linear"], done["attended"])
 

time: 284 us -> 332 us (1.17)
  the two profiles are of different devices: /device:TPU:31 before, /device:TPU:25 now
where the time goes in v3:
time: 332 us; the launch traced here: 326 us
  Pallas kernels  124 us (37%)
  waiting for transfers between devices  105 us (32%)
  starting transfers between devices  54.2 us (16%)
  matrix products  15.9 us (5%)
  between operations  14.5 us (4%)
  local copies, waits for them, and re-layouts  10.2 us (3%)
    ppermute x21, waiting for transfers between devices, moved(): lax.ppermute(value, 'ctx', [(s, t) for s, t in pairs if 0 <= t < count])  105 us
    ppermute x21, starting transfers between devices, moved(): lax.ppermute(value, 'ctx', [(s, t) for s, t in pairs if 0 <= t < count])  54.2 us
    pallas_call x4, Pallas kernels, attend(): pl.pallas_call(attend_kernel, grid_spec=pltpu.PrefetchScalarGridSpec(num_...  51.8 us
    dot_general x1, matrix products, do_project(): jnp.dot(light['normed'], out_weight, preferred_element_type=jnp.float32)  15.9 us
    pallas_call x4, Pallas kernels, pick(): pl.pallas_call(pick_kernel, grid_spec=pltpu.PrefetchScalarGridSpec(num_sc...  14.7 us
    pallas_call x1, Pallas kernels, mix_local(): pl.pallas_call(mix_local_kernel, grid=(width // WIDE,), in_specs=[block,...  14.3 us
    pallas_call x1, Pallas kernels, mix_final(): pl.pallas_call(functools.partial(mix_final_kernel, half), grid_spec=pltpu...  11.3 us
    pallas_call x4, Pallas kernels, pack(): pl.pallas_call(pack_kernel, grid=(bundles,), in_specs=[block, block] + un...  10.8 us
  transfers between devices with their start and end apart: 22, of which 8 were waited for; matrix products, arithmetic and copies ran while one was open for 1% of the time, Pallas kernels for 34%

profile of v3, /device:TPU:25, one launch (start us, length us, event | category | flops | bytes accessed | tf_op | source)
XLA Modules:
  0.0 325.9 jit_solution(4106775694579008924)
XLA Ops:
  7.2 0.0 copy-start
  7.2 0.0 reduce-scatter.2.cloned.1.call-start
  7.2 2.3 pack.4.rest_0_
  9.6 1.3 collective-permute-start.1
  10.9 4.3 %collective-permute-start.2 = (bf16[2,512,768]{2,1,0:T(8,128)(2,1)}, bf16[2,512,768]{2,1,0:T(8,128)(2,1)}, u32[]{:S(2)}, u32[]{:S(2)}) collective-permute-start(bf16[2,512,768]{2,1,0:T(8,128)(2,1)} %pack.4.rest_0_), channel_id=1, source_target_pairs={{0,4},{2,6},{4,8},{8,12},{10,14},{12,16},{16,20},{18,22},{20,24},{... | collective-permute-start | bytes 4718600 | tf_op jit(solution)/shard_map/ppermute | solution.py:492
  15.1 3.9 %pack.5.rest_0_ = bf16[2,512,1152]{2,1,0:T(8,128)(2,1)} custom-call(bf16[512,3072]{1,0:T(8,128)(2,1)} %key_ref.19, bf16[512,3072]{1,0:T(8,128)(2,1)} %value_ref.19, bf16[2,512,768]{2,1,0:T(8,128)(2,1)} %pack.4.rest_0_), custom_call_target="tpu_custom_call" | custom-call | flops 1000 | bytes 1000 | tf_op jit(solution)/shard_map/pack/pallas_call | solution.py:64
  19.1 1.3 collective-permute-start.7
  20.4 1.2 reduce-window.6
  21.5 0.2 slice_reduce_fusion
  21.7 0.1 broadcast_add_fusion
  21.9 0.7 reduce_window_sum.21.decay_ref.row_ref
  22.5 9.3 %local_state.1 = (f32[32,96,128]{2,1,0:T(8,128)}, f32[32,96,128]{2,1,0:T(8,128)}, bf16[32,96,128]{2,1,0:T(8,128)(2,1)}) custom-call(bf16[512,3072]{1,0:T(8,128)(2,1)} %key_ref.13, bf16[512,3072]{1,0:T(8,128)(2,1)} %value_ref.13, f32[8,4,512]{2,1,0:T(4,128)} %reduce_window_sum.21.decay_ref.row_ref, bf16[2,512,1152]{2,1,0:T(8,128)(2,1)} %pack.5.rest_0_), custom_call_target="tpu_custom_call" | custom-call | flops 1000 | bytes 1000 | tf_op jit(solution)/shard_map/local_state/pallas_call | solution.py:286
  31.8 0.1 bitcast_bitcast_fusion
  32.0 2.0 copy.21
  33.9 14.3 %mix_local.1.refs_1_.local_ref = f32[3072,512]{1,0:T(8,128)} custom-call(bf16[512,3072]{1,0:T(8,128)(2,1)} %query_ref.8, bf16[512,3072]{1,0:T(8,128)(2,1)} %key_ref.13, bf16[512,3072]{1,0:T(8,128)(2,1)} %value_ref.13, f32[8,512,4]{2,1,0:T(8,128)} %bitcast.19, f32[8,4,512]{2,1,0:T(4,128)} %reduce_window_sum.21.decay_ref.row_ref, ...), custom_call_target="tpu_custom_call" | custom-call | flops 1000 | bytes 1000 | tf_op jit(solution)/shard_map/mix_local/pallas_call | solution.py:407
  48.3 1.3 collective-permute-start.4
  49.6 1.6 collective-permute-start
  51.2 5.3 %collective-permute-start.8 = (bf16[2,512,1152]{2,1,0:T(8,128)(2,1)}, bf16[2,512,1152]{2,1,0:T(8,128)(2,1)}, u32[]{:S(2)}, u32[]{:S(2)}) collective-permute-start(bf16[2,512,1152]{2,1,0:T(8,128)(2,1)} %pack.5.rest_0_), channel_id=1, source_target_pairs={{0,4},{2,6},{4,8},{8,12},{10,14},{12,16},{16,20},{18,22},{20,24},{... | collective-permute-start | bytes 7077896 | tf_op jit(solution)/shard_map/ppermute | solution.py:492
  56.5 0.9 copy-done.4
  57.4 2.7 chip_state.1
  60.1 1.9 collective-permute-start.3
  62.0 19.3 %collective-permute-done.4.back_ref = bf16[2,512,768]{2,1,0:T(8,128)(2,1)} collective-permute-done((bf16[2,512,768]{2,1,0:T(8,128)(2,1)}, bf16[2,512,768]{2,1,0:T(8,128)(2,1)}, u32[]{:S(2)}, u32[]{:S(2)}) %collective-permute-start.4) | collective-permute-done | bytes 1572896 | tf_op jit(solution)/shard_map/ppermute | solution.py:492
  81.3 3.7 %pick.4.rest_0_.mid_ref = bf16[2,512,768]{2,1,0:T(8,128)(2,1)} custom-call(s32[1]{0:T(128)} %bitcast.info, bf16[2,512,768]{2,1,0:T(8,128)(2,1)} %collective-permute-done.2.rest_1_.chip_ref, bf16[2,512,768]{2,1,0:T(8,128)(2,1)} %collective-permute-done.4.back_ref, bf16[16,96,128]{2,1,0:T(8,128)(2,1)} %get-tuple-element.19.rest_0_), custom_call_target="tpu_custom_call" | custom-call | flops 1000 | bytes 1000 | tf_op jit(solution)/shard_map/pick/pallas_call | solution.py:101
  85.1 29.4 %collective-permute-done.3.arrived_ref = bf16[16,96,128]{2,1,0:T(8,128)(2,1)S(1)} collective-permute-done((bf16[16,96,128]{2,1,0:T(8,128)(2,1)}, bf16[16,96,128]{2,1,0:T(8,128)(2,1)S(1)}, u32[]{:S(2)}, u32[]{:S(2)}) %collective-permute-start.3) | collective-permute-done | bytes 393248 | tf_op jit(solution)/shard_map/ppermute | solution.py:492
  114.5 0.8 copy-done.10
  115.3 3.3 %join.3 = (f32[16,96,128]{2,1,0:T(8,128)}, f32[16,96,128]{2,1,0:T(8,128)}, bf16[16,96,128]{2,1,0:T(8,128)(2,1)}) custom-call(f32[16,96,128]{2,1,0:T(8,128)} %get-tuple-element.18.chip_ref.before_ref, f32[16,96,128]{2,1,0:T(8,128)} %get-tuple-element.18.chip_ref.before_ref, bf16[16,96,128]{2,1,0:T(8,128)(2,1)} %copy-done.10, ...), custom_call_target="tpu_custom_call" | custom-call | flops 1000 | bytes 1000 | tf_op jit(solution)/shard_map/join/pallas_call | solution.py:353
  118.6 1.4 collective-permute-start.10
  120.0 1.5 collective-permute-start.5
  121.5 12.9 %attend.4.rest_0_ = bf16[512,3072]{1,0:T(8,128)(2,1)} custom-call(s32[1]{0:T(128)} %bitcast.info, bf16[512,3072]{1,0:T(8,128)(2,1)} %query_ref.11, bf16[512,3072]{1,0:T(8,128)(2,1)} %key_ref.19, bf16[512,3072]{1,0:T(8,128)(2,1)} %value_ref.19, bf16[2,512,768]{2,1,0:T(8,128)(2,1)} %gate.4.rest_0_.near_ref, bf16[2,512,768]{2,1,0:T(8,128)(2,1)} %pick.4.rest_0_.mid_ref, ...), custom_call_target="tpu_custom_call" | custom-call | flops 1000 | bytes 1000 | tf_op jit(solution)/shard_map/attend/pallas_call | solution.py:210
  134.4 0.7 copy-done.7
  135.2 3.1 join.4
  138.3 2.4 pack.6.rest_0_
  140.8 5.9 %collective-permute-start.12 = (bf16[2,512,768]{2,1,0:T(8,128)(2,1)}, bf16[2,512,768]{2,1,0:T(8,128)(2,1)}, u32[]{:S(2)}, u32[]{:S(2)}) collective-permute-start(bf16[2,512,768]{2,1,0:T(8,128)(2,1)} %pack.6.rest_0_), channel_id=1, source_target_pairs={{0,4},{2,6},{4,8},{8,12},{10,14},{12,16},{16,20},{18,22},{20,24},{... | collective-permute-start | bytes 4718600 | tf_op jit(solution)/shard_map/ppermute | solution.py:492
  146.7 1.7 collective-permute-start.9
  148.4 1.2 collective-permute-done.10.back_ref
  149.6 5.2 %pick.5.rest_0_.mid_ref = bf16[2,512,1152]{2,1,0:T(8,128)(2,1)} custom-call(s32[1]{0:T(128)} %bitcast.info, bf16[2,512,1152]{2,1,0:T(8,128)(2,1)} %collective-permute-done.8.rest_1_.chip_ref, bf16[2,512,1152]{2,1,0:T(8,128)(2,1)} %collective-permute-done.10.back_ref, bf16[2,512,768]{2,1,0:T(8,128)(2,1)} %pack.6.rest_0_), custom_call_target="tpu_custom_call" | custom-call | flops 1000 | bytes 1000 | tf_op jit(solution)/shard_map/pick/pallas_call | solution.py:101
  154.7 15.5 %collective-permute-done.9.arrived_ref = bf16[16,96,128]{2,1,0:T(8,128)(2,1)S(1)} collective-permute-done((bf16[16,96,128]{2,1,0:T(8,128)(2,1)S(1)}, bf16[16,96,128]{2,1,0:T(8,128)(2,1)S(1)}, u32[]{:S(2)}, u32[]{:S(2)}) %collective-permute-start.9) | collective-permute-done | bytes 393248 | tf_op jit(solution)/shard_map/ppermute | solution.py:492
  170.2 0.7 copy-done.11
  170.9 3.0 join.5
  173.9 1.3 collective-permute-start.11
  175.2 2.1 pack.7.rest_0_
  177.3 0.8 collective-permute-done.12.rest_1_.chip_ref
  178.1 11.3 %mix_final.1.refs_1_ = bf16[512,3072]{1,0:T(8,128)(2,1)} custom-call(s32[1]{0:T(128)} %bitcast.info, bf16[512,3072]{1,0:T(8,128)(2,1)} %query_ref.8, f32[3072,512]{1,0:T(8,128)} %mix_local.1.refs_1_.local_ref, f32[8,4,512]{2,1,0:T(4,128)} %reduce_window_sum.21.decay_ref.row_ref, f32[16,96,128]{2,1,0:T(8,128)} %get-tuple-element.26.own_ref, ...), custom_call_target="tpu_custom_call" | custom-call | flops 1000 | bytes 1000 | tf_op jit(solution)/shard_map/mix_final/pallas_call | solution.py:455
  189.4 15.9 %convolution_convert_fusion.refs_1_ = bf16[512,3072]{1,0:T(8,128)(2,1)} fusion(bf16[512,3072]{1,0:T(8,128)(2,1)} %mix_final.1.refs_1_, bf16[3072,3072]{1,0:T(8,128)(2,1)} %param.12), kind=kOutput, calls=%fused_computation | convolution fusion | flops 9665249280 | bytes 25165824 | tf_op jit(solution)/shard_map/dot_general | solution.py:581
  205.3 0.0 reduce-scatter.2.cloned.1.call-update
  205.3 1.4 copy-done.3
  206.7 1.3 collective-permute-start.17
  208.0 3.0 collective-permute-start.16
  211.0 4.2 %collective-permute-done.17.refs_0_ = bf16[2,512,768]{2,1,0:T(8,128)(2,1)} collective-permute-done((bf16[2,512,768]{2,1,0:T(8,128)(2,1)S(1)}, bf16[2,512,768]{2,1,0:T(8,128)(2,1)}, u32[]{:S(2)}, u32[]{:S(2)}) %collective-permute-start.17) | collective-permute-done | bytes 1572896 | tf_op jit(solution)/shard_map/ppermute | solution.py:492
  215.2 1.3 collective-permute-start.18
  216.5 1.3 collective-permute-start.13
  217.8 16.6 %collective-permute-start.14 = (bf16[2,512,384]{2,1,0:T(8,128)(2,1)}, bf16[2,512,384]{2,1,0:T(8,128)(2,1)}, u32[]{:S(2)}, u32[]{:S(2)}) collective-permute-start(bf16[2,512,384]{2,1,0:T(8,128)(2,1)} %pack.7.rest_0_), channel_id=1, source_target_pairs={{0,4},{2,6},{4,8},{8,12},{10,14},{12,16},{16,20},{18,22},{20,24},{... | collective-permute-start | bytes 2359304 | tf_op jit(solution)/shard_map/ppermute | solution.py:492
  234.4 2.3 collective-permute-done.13.refs_0_
  236.8 0.9 copy-done.2
  237.7 1.3 collective-permute-start.15
  239.0 32.6 %collective-permute-done.18.back_ref = bf16[2,512,768]{2,1,0:T(8,128)(2,1)} collective-permute-done((bf16[2,512,768]{2,1,0:T(8,128)(2,1)}, bf16[2,512,768]{2,1,0:T(8,128)(2,1)}, u32[]{:S(2)}, u32[]{:S(2)}) %collective-permute-start.18) | collective-permute-done | bytes 1572896 | tf_op jit(solution)/shard_map/ppermute | solution.py:492
  271.6 3.8 %pick.6.rest_1_.mid_ref = bf16[2,512,768]{2,1,0:T(8,128)(2,1)} custom-call(s32[1]{0:T(128)} %bitcast.info, bf16[2,512,768]{2,1,0:T(8,128)(2,1)} %collective-permute-done.12.rest_1_.chip_ref, bf16[2,512,768]{2,1,0:T(8,128)(2,1)} %collective-permute-done.18.back_ref, bf16[2,512,384]{2,1,0:T(8,128)(2,1)} %gate.6.rest_0_.near_ref), custom_call_target="tpu_custom_call" | custom-call | flops 1000 | bytes 1000 | tf_op jit(solution)/shard_map/pick/pallas_call | solution.py:101
  275.4 18.0 %attend.5.rest_0_ = bf16[512,3072]{1,0:T(8,128)(2,1)} custom-call(s32[1]{0:T(128)} %bitcast.info, bf16[512,3072]{1,0:T(8,128)(2,1)} %query_ref.11, bf16[512,3072]{1,0:T(8,128)(2,1)} %key_ref.19, bf16[512,3072]{1,0:T(8,128)(2,1)} %value_ref.19, bf16[2,512,1152]{2,1,0:T(8,128)(2,1)} %gate.5.rest_0_.near_ref, ...), custom_call_target="tpu_custom_call", output_to_operand_aliasing={{}: (7, {})} | custom-call | flops 1000 | bytes 1000 | tf_op jit(solution)/shard_map/attend/pallas_call | solution.py:210
  293.4 0.9 copy-done.5
  294.3 2.1 pick.7.rest_1_.mid_ref
  296.4 0.5 collective-permute-start.19
  296.9 13.0 %attend.6.rest_0_ = bf16[512,3072]{1,0:T(8,128)(2,1)} custom-call(s32[1]{0:T(128)} %bitcast.info, bf16[512,3072]{1,0:T(8,128)(2,1)} %query_ref.11, bf16[512,3072]{1,0:T(8,128)(2,1)} %key_ref.19, bf16[512,3072]{1,0:T(8,128)(2,1)} %value_ref.19, bf16[2,512,768]{2,1,0:T(8,128)(2,1)} %gate.7.near_ref, ...), custom_call_target="tpu_custom_call", output_to_operand_aliasing={{}: (7, {})} | custom-call | flops 1000 | bytes 1000 | tf_op jit(solution)/shard_map/attend/pallas_call | solution.py:210
  309.9 0.9 copy-done.6
  310.9 8.0 %attend.7 = bf16[512,3072]{1,0:T(8,128)(2,1)} custom-call(s32[1]{0:T(128)} %bitcast.info, bf16[512,3072]{1,0:T(8,128)(2,1)} %query_ref.11, bf16[512,3072]{1,0:T(8,128)(2,1)} %key_ref.19, bf16[512,3072]{1,0:T(8,128)(2,1)} %value_ref.19, bf16[2,512,384]{2,1,0:T(8,128)(2,1)} %gate.6.rest_0_.near_ref, ...), custom_call_target="tpu_custom_call", output_to_operand_aliasing={{}: (7, {})} | custom-call | flops 1000 | bytes 1000 | tf_op jit(solution)/shard_map/attend/pallas_call | solution.py:210
  (42 shorter events, 0.2 us)
Async XLA Ops:
  7.2 13.2 %copy-start = (f32[512,32]{0,1:T(8,128)S(1)}, f32[512,32]{0,1:T(8,128)}, u32[]{:S(2)}) copy-start(f32[512,32]{0,1:T(8,128)} %param.11) | copy-start | bytes 196612
  7.2 311.6 %reduce-scatter.2.cloned.1.call-start = ((), (), s32[]{:S(2)}) async-start(), calls=%async_computation.1 | async-start | bytes 4718592 | tf_op jit(solution)/shard_map/reduce_scatter | solution.py:583
  9.6 38.7 %collective-permute-start.1 = (bf16[2,512,768]{2,1,0:T(8,128)(2,1)}, bf16[2,512,768]{2,1,0:T(8,128)(2,1)}, u32[]{:S(2)}, u32[]{:S(2)}) collective-permute-start(bf16[2,512,768]{2,1,0:T(8,128)(2,1)} %pack.4.rest_0_), channel_id=1, source_target_pairs={{0,2},{2,8},{4,6},{6,12},{8,10},{10,16},{12,14},{14,20},{16,18},{1... | collective-permute-start | bytes 4718600 | tf_op jit(solution)/shard_map/ppermute | solution.py:492
  10.9 45.7 %collective-permute-start.2 = (bf16[2,512,768]{2,1,0:T(8,128)(2,1)}, bf16[2,512,768]{2,1,0:T(8,128)(2,1)}, u32[]{:S(2)}, u32[]{:S(2)}) collective-permute-start(bf16[2,512,768]{2,1,0:T(8,128)(2,1)} %pack.4.rest_0_), channel_id=1, source_target_pairs={{0,4},{2,6},{4,8},{8,12},{10,14},{12,16},{16,20},{18,22},{20,24},{... | collective-permute-start | bytes 4718600 | tf_op jit(solution)/shard_map/ppermute | solution.py:492
  19.1 99.5 %collective-permute-start.7 = (bf16[2,512,1152]{2,1,0:T(8,128)(2,1)}, bf16[2,512,1152]{2,1,0:T(8,128)(2,1)}, u32[]{:S(2)}, u32[]{:S(2)}) collective-permute-start(bf16[2,512,1152]{2,1,0:T(8,128)(2,1)} %pack.5.rest_0_), channel_id=1, source_target_pairs={{0,2},{2,8},{4,6},{6,12},{8,10},{10,16},{12,14},{14,20},{16,18},{1... | collective-permute-start | bytes 7077896 | tf_op jit(solution)/shard_map/ppermute | solution.py:492
  48.3 33.1 %collective-permute-start.4 = (bf16[2,512,768]{2,1,0:T(8,128)(2,1)}, bf16[2,512,768]{2,1,0:T(8,128)(2,1)}, u32[]{:S(2)}, u32[]{:S(2)}) collective-permute-start(bf16[2,512,768]{2,1,0:T(8,128)(2,1)} %gate.4.rest_0_.near_ref), channel_id=1, source_target_pairs={{12,10},{20,18},{28,26},{13,11},{21,19},{29,27}} | collective-permute-start | bytes 4718600 | tf_op jit(solution)/shard_map/ppermute | solution.py:492
  49.6 7.0 %collective-permute-start = (bf16[32,96,128]{2,1,0:T(8,128)(2,1)}, bf16[32,96,128]{2,1,0:T(8,128)(2,1)S(1)}, u32[]{:S(2)}, u32[]{:S(2)}) collective-permute-start(bf16[32,96,128]{2,1,0:T(8,128)(2,1)} %get-tuple-element.16.rest_0_), channel_id=1, source_target_pairs={{0,2},{2,0},{4,6},{6,4},{8,10},{10,8},{12,14},{14,12},{16,18},{18,... | collective-permute-start | bytes 2359304 | tf_op jit(solution)/shard_map/ppermute | solution.py:492
  51.2 83.2 %collective-permute-start.8 = (bf16[2,512,1152]{2,1,0:T(8,128)(2,1)}, bf16[2,512,1152]{2,1,0:T(8,128)(2,1)}, u32[]{:S(2)}, u32[]{:S(2)}) collective-permute-start(bf16[2,512,1152]{2,1,0:T(8,128)(2,1)} %pack.5.rest_0_), channel_id=1, source_target_pairs={{0,4},{2,6},{4,8},{8,12},{10,14},{12,16},{16,20},{18,22},{20,24},{... | collective-permute-start | bytes 7077896 | tf_op jit(solution)/shard_map/ppermute | solution.py:492
  56.5 0.9 copy-start.4
  60.1 54.4 %collective-permute-start.3 = (bf16[16,96,128]{2,1,0:T(8,128)(2,1)}, bf16[16,96,128]{2,1,0:T(8,128)(2,1)S(1)}, u32[]{:S(2)}, u32[]{:S(2)}) collective-permute-start(bf16[16,96,128]{2,1,0:T(8,128)(2,1)} %get-tuple-element.19.rest_0_), channel_id=1, source_target_pairs={{0,4},{2,6},{4,8},{6,10},{8,12},{10,14},{12,16},{14,18},{16,20},{1... | collective-permute-start | bytes 1179656 | tf_op jit(solution)/shard_map/ppermute | solution.py:492
  85.1 36.5 %collective-permute-start.6 = (bf16[2,512,768]{2,1,0:T(8,128)(2,1)}, bf16[2,512,768]{2,1,0:T(8,128)(2,1)}, u32[]{:S(2)}, u32[]{:S(2)}) collective-permute-start(bf16[2,512,768]{2,1,0:T(8,128)(2,1)} %pick.4.rest_0_.mid_ref), channel_id=1, source_target_pairs={{0,2},{2,0},{4,6},{6,4},{8,10},{10,8},{12,14},{14,12},{16,18},{18,... | collective-permute-start | bytes 4718600 | tf_op jit(solution)/shard_map/ppermute | solution.py:492
  114.5 0.8 copy-start.10
  118.6 1.4 copy-start.9
  118.6 31.0 %collective-permute-start.10 = (bf16[2,512,1152]{2,1,0:T(8,128)(2,1)}, bf16[2,512,1152]{2,1,0:T(8,128)(2,1)}, u32[]{:S(2)}, u32[]{:S(2)}) collective-permute-start(bf16[2,512,1152]{2,1,0:T(8,128)(2,1)} %gate.5.rest_0_.near_ref), channel_id=1, source_target_pairs={{12,10},{20,18},{28,26},{13,11},{21,19},{29,27}} | collective-permute-start | bytes 7077896 | tf_op jit(solution)/shard_map/ppermute | solution.py:492
  120.0 14.4 %collective-permute-start.5 = (bf16[16,96,128]{2,1,0:T(8,128)(2,1)S(1)}, bf16[16,96,128]{2,1,0:T(8,128)(2,1)S(1)}, u32[]{:S(2)}, u32[]{:S(2)}) collective-permute-start(bf16[16,96,128]{2,1,0:T(8,128)(2,1)S(1)} %copy-done.9), channel_id=1, source_target_pairs={{0,8},{2,10},{4,12},{6,14},{8,16},{10,18},{12,20},{14,22},{16,24},... | collective-permute-start | bytes 1179656 | tf_op jit(solution)/shard_map/ppermute | solution.py:492
  134.4 0.8 copy-start.7
  138.3 8.4 %copy-start.8 = (bf16[16,96,128]{2,1,0:T(8,128)(2,1)S(1)}, bf16[16,96,128]{2,1,0:T(8,128)(2,1)}, u32[]{:S(2)}) copy-start(bf16[16,96,128]{2,1,0:T(8,128)(2,1)} %get-tuple-element.25.rest_0_) | copy-start | bytes 1179652
  140.8 37.3 %collective-permute-start.12 = (bf16[2,512,768]{2,1,0:T(8,128)(2,1)}, bf16[2,512,768]{2,1,0:T(8,128)(2,1)}, u32[]{:S(2)}, u32[]{:S(2)}) collective-permute-start(bf16[2,512,768]{2,1,0:T(8,128)(2,1)} %pack.6.rest_0_), channel_id=1, source_target_pairs={{0,4},{2,6},{4,8},{8,12},{10,14},{12,16},{16,20},{18,22},{20,24},{... | collective-permute-start | bytes 4718600 | tf_op jit(solution)/shard_map/ppermute | solution.py:492
  146.7 23.5 %collective-permute-start.9 = (bf16[16,96,128]{2,1,0:T(8,128)(2,1)S(1)}, bf16[16,96,128]{2,1,0:T(8,128)(2,1)S(1)}, u32[]{:S(2)}, u32[]{:S(2)}) collective-permute-start(bf16[16,96,128]{2,1,0:T(8,128)(2,1)S(1)} %copy-done.8), channel_id=1, source_target_pairs={{0,16},{2,18},{4,20},{6,22},{8,24},{10,26},{12,28},{14,30},{1,17},... | collective-permute-start | bytes 1179656 | tf_op jit(solution)/shard_map/ppermute | solution.py:492
  170.2 0.7 copy-start.11
  173.9 3.4 %collective-permute-start.11 = (bf16[16,96,128]{2,1,0:T(8,128)(2,1)}, bf16[16,96,128]{2,1,0:T(8,128)(2,1)S(1)}, u32[]{:S(2)}, u32[]{:S(2)}) collective-permute-start(bf16[16,96,128]{2,1,0:T(8,128)(2,1)} %get-tuple-element.27.rest_0_), channel_id=1, source_target_pairs={{0,2},{2,0},{4,6},{6,4},{8,10},{10,8},{12,14},{14,12},{16,18},{18,... | collective-permute-start | bytes 1179656 | tf_op jit(solution)/shard_map/ppermute | solution.py:492
  177.3 0.8 copy-start.12
  205.3 1.4 copy-start.3
  206.7 8.6 %collective-permute-start.17 = (bf16[2,512,768]{2,1,0:T(8,128)(2,1)S(1)}, bf16[2,512,768]{2,1,0:T(8,128)(2,1)}, u32[]{:S(2)}, u32[]{:S(2)}) collective-permute-start(bf16[2,512,768]{2,1,0:T(8,128)(2,1)S(1)} %copy-done.3), channel_id=1, source_target_pairs={{0,2},{2,8},{4,6},{6,12},{8,10},{10,16},{12,14},{14,20},{16,18},{1... | collective-permute-start | bytes 4718600 | tf_op jit(solution)/shard_map/ppermute | solution.py:492
  208.0 67.4 %collective-permute-start.16 = (bf16[2,512,1152]{2,1,0:T(8,128)(2,1)}, bf16[2,512,1152]{2,1,0:T(8,128)(2,1)}, u32[]{:S(2)}, u32[]{:S(2)}) collective-permute-start(bf16[2,512,1152]{2,1,0:T(8,128)(2,1)} %pick.5.rest_0_.mid_ref), channel_id=1, source_target_pairs={{0,2},{2,0},{4,6},{6,4},{8,10},{10,8},{12,14},{14,12},{16,18},{18,... | collective-permute-start | bytes 7077896 | tf_op jit(solution)/shard_map/ppermute | solution.py:492
  215.2 56.4 %collective-permute-start.18 = (bf16[2,512,768]{2,1,0:T(8,128)(2,1)}, bf16[2,512,768]{2,1,0:T(8,128)(2,1)}, u32[]{:S(2)}, u32[]{:S(2)}) collective-permute-start(bf16[2,512,768]{2,1,0:T(8,128)(2,1)} %gate.7.near_ref), channel_id=1, source_target_pairs={{12,10},{20,18},{28,26},{13,11},{21,19},{29,27}} | collective-permute-start | bytes 4718600 | tf_op jit(solution)/shard_map/ppermute | solution.py:492
  216.5 20.2 %collective-permute-start.13 = (bf16[2,512,384]{2,1,0:T(8,128)(2,1)}, bf16[2,512,384]{2,1,0:T(8,128)(2,1)S(1)}, u32[]{:S(2)}, u32[]{:S(2)}) collective-permute-start(bf16[2,512,384]{2,1,0:T(8,128)(2,1)} %pack.7.rest_0_), channel_id=1, source_target_pairs={{0,2},{2,8},{4,6},{6,12},{8,10},{10,16},{12,14},{14,20},{16,18},{1... | collective-permute-start | bytes 2359304 | tf_op jit(solution)/shard_map/ppermute | solution.py:492
  217.8 75.5 %collective-permute-start.14 = (bf16[2,512,384]{2,1,0:T(8,128)(2,1)}, bf16[2,512,384]{2,1,0:T(8,128)(2,1)}, u32[]{:S(2)}, u32[]{:S(2)}) collective-permute-start(bf16[2,512,384]{2,1,0:T(8,128)(2,1)} %pack.7.rest_0_), channel_id=1, source_target_pairs={{0,4},{2,6},{4,8},{8,12},{10,14},{12,16},{16,20},{18,22},{20,24},{... | collective-permute-start | bytes 2359304 | tf_op jit(solution)/shard_map/ppermute | solution.py:492
  236.8 0.9 copy-start.2
  237.7 55.7 %collective-permute-start.15 = (bf16[2,512,384]{2,1,0:T(8,128)(2,1)}, bf16[2,512,384]{2,1,0:T(8,128)(2,1)S(1)}, u32[]{:S(2)}, u32[]{:S(2)}) collective-permute-start(bf16[2,512,384]{2,1,0:T(8,128)(2,1)} %gate.6.rest_0_.near_ref), channel_id=1, source_target_pairs={{12,10},{20,18},{28,26},{13,11},{21,19},{29,27}} | collective-permute-start | bytes 2359304 | tf_op jit(solution)/shard_map/ppermute | solution.py:492
  275.4 21.5 %collective-permute-start.20 = (bf16[2,512,768]{2,1,0:T(8,128)(2,1)}, bf16[2,512,768]{2,1,0:T(8,128)(2,1)}, u32[]{:S(2)}, u32[]{:S(2)}) collective-permute-start(bf16[2,512,768]{2,1,0:T(8,128)(2,1)} %pick.6.rest_1_.mid_ref), channel_id=1, source_target_pairs={{0,2},{2,0},{4,6},{6,4},{8,10},{10,8},{12,14},{14,12},{16,18},{18,... | collective-permute-start | bytes 4718600 | tf_op jit(solution)/shard_map/ppermute | solution.py:492
  293.4 0.9 copy-start.5
  296.4 13.5 %collective-permute-start.19 = (bf16[2,512,384]{2,1,0:T(8,128)(2,1)}, bf16[2,512,384]{2,1,0:T(8,128)(2,1)S(1)}, u32[]{:S(2)}, u32[]{:S(2)}) collective-permute-start(bf16[2,512,384]{2,1,0:T(8,128)(2,1)} %pick.7.rest_1_.mid_ref), channel_id=1, source_target_pairs={{0,2},{2,0},{4,6},{6,4},{8,10},{10,8},{12,14},{14,12},{16,18},{18,... | collective-permute-start | bytes 2359304 | tf_op jit(solution)/shard_map/ppermute | solution.py:492
  309.9 0.9 copy-start.6
  310.9 8.0 %copy-start.1 = (f32[512,32]{0,1:T(8,128)S(1)}, f32[512,32]{0,1:T(8,128)}, u32[]{:S(2)}) copy-start(f32[512,32]{0,1:T(8,128)} %param.11) | copy-start | bytes 196612
Sparse Core Ops, SparseCore 0:
  205.4 57.6 reduce-scatter.1
